TPU v7x, 32 devices: a whole 2x2x4 slice. The times are simulated.
32 devices in a mesh: ctx: 8 (over y, x, core), dp: 4 (over z).
Axes of the slice: x: 2, y: 2, z: 4, core: 2. Of those that a mesh axis runs over, the one named last changes fastest.
Arguments:
- tokens: bfloat16 [4, 1024, 1536], P('dp', 'ctx'), may hold values from -6 to 6
- w_in: bfloat16 [1536, 2880], replicated, may hold values from -0.15625 to 0.15625
- conv_taps: float32 [7, 2880], replicated, may hold values from -2.4 to 2.4
- residues: float32 [960, 16], P('ctx'), may hold values from -1.5 to 1.5
- rates: float32 [960, 16], P('ctx'), may hold values from 0.00029296875 to 0.08
- cotangent: bfloat16 [4, 1024, 960], P('dp', 'ctx'), may hold values from -6 to 6
Outputs:
- output: bfloat16 [4, 1024, 960], P('dp', 'ctx')
- grad_tokens: bfloat16 [4, 1024, 1536], P('dp', 'ctx')
- grad_weight: bfloat16 [1536, 2880], P('ctx', 'dp')
- grad_taps: float32 [7, 2880], replicated
- grad_residues: float32 [960, 16], P('ctx')
All inputs are finite; a program needn't handle non-finite values.
Results may differ from a plain program's by a relative error of at most 0.02.
Values may be sent and summed in bfloat16 or wider, within the bound.
A program may use at most 192 MiB of HBM per device.

v0:
```python
import math

import jax
import jax.numpy as jnp
from jax import lax
from jax.sharding import PartitionSpec as P

BLK = 128


precise = lax.Precision.HIGH


def shifted(block, axis, distance):
    devices = range(lax.axis_size(axis))
    route = [(i - distance, i) for i in devices if i - distance in devices]
    return lax.ppermute(block, axis, route)


def powers(rates, offsets):
    return jnp.exp(-rates[:, :, None] * offsets[None, None, :])


def mixed_dot(form, data, factor):
    upper = factor.astype(jnp.bfloat16)
    lower = (factor - upper.astype(jnp.float32)).astype(jnp.bfloat16)
    first = jnp.einsum(form, data, upper, preferred_element_type=jnp.float32)
    return first + jnp.einsum(form, data, lower, preferred_element_type=jnp.float32)


def lag_matrix(reff, rates, blk):
    pos = jnp.arange(blk).astype(jnp.float32)
    lagged = jnp.einsum("ck,ckn->cn", reff, powers(rates, pos), precision=precise)
    index = jnp.arange(blk)[:, None] - jnp.arange(blk)[None, :]
    return jnp.where(index[None] >= 0, lagged[:, jnp.maximum(index, 0)], 0.0)


def block_links(rates, count, blk):
    order = jnp.arange(count)
    gap = order[:, None] - order[None, :] - 1
    depth = (blk * jnp.maximum(gap, 0)).astype(jnp.float32)
    return jnp.where(
        gap[None, None] >= 0, jnp.exp(-rates[:, :, None, None] * depth[None, None]), 0.0
    )


def forward_local(u3, reff, rates, incoming):
    count, blk = (u3.shape[1], u3.shape[2])
    pos = jnp.arange(blk).astype(jnp.float32)
    inner = mixed_dot("cbj,cij->cbi", u3, lag_matrix(reff, rates, blk))
    ends = mixed_dot("cbj,ckj->ckb", u3, powers(rates, blk - 1.0 - pos))
    entry = powers(rates, (blk * jnp.arange(count)).astype(jnp.float32))
    starts = jnp.einsum("ckbd,ckd->ckb", block_links(rates, count, blk), ends, precision=precise)
    starts = starts + entry * incoming[:, :, None]
    outer = jnp.einsum(
        "ckb,cki->cbi", reff[:, :, None] * starts, powers(rates, pos + 1.0), precision=precise
    )
    return (inner + outer, starts)


def backward_local(g3, u3, reff, rates, starts, later):
    count, blk = (g3.shape[1], g3.shape[2])
    pos = jnp.arange(blk).astype(jnp.float32)
    inner = mixed_dot("cbi,cij->cbj", g3, lag_matrix(reff, rates, blk))
    heads = mixed_dot("cbi,cki->ckb", g3, powers(rates, pos))
    exits = powers(rates, (blk * (count - 1 - jnp.arange(count))).astype(jnp.float32))
    tails = jnp.einsum("ckdb,ckd->ckb", block_links(rates, count, blk), heads, precision=precise)
    tails = tails + exits * later[:, :, None]
    outer = jnp.einsum(
        "ckb,ckj->cbj", reff[:, :, None] * tails, powers(rates, blk - pos), precision=precise
    )
    cross = jnp.sum(starts * heads, axis=2) * jnp.exp(-rates)
    pair = jnp.einsum("cbi,cbj->cij", g3, u3, preferred_element_type=jnp.float32)
    index = jnp.arange(blk)[:, None] - jnp.arange(blk)[None, :]
    pair = jnp.where(index[None] >= 0, pair, 0.0)
    near = jnp.einsum(
        "cij,ckj->cki", pair, jnp.exp(rates[:, :, None] * pos[None, None, :]), precision=precise
    )
    near = jnp.sum(near * powers(rates, pos), axis=2)
    return (inner + outer, cross + near)


def grouped(func, arrays):
    chans = arrays[0].shape[0]
    blk = arrays[0].shape[-1]
    groups = max(1, chans * blk * blk // (1 << 22))
    while chans % groups:
        groups = groups + 1
    split = tuple((a.reshape((groups, chans // groups) + a.shape[1:]) for a in arrays))
    results = lax.map(lambda items: func(*items), split)
    return tuple((r.reshape((chans,) + r.shape[2:]) for r in results))


def local(tokens, w_in, conv_taps, residues, rates, cotangent):
    rim = conv_taps.shape[0] - 1
    feats = tokens[0]
    rows = feats.shape[0]
    width = cotangent.shape[2]
    modes = rates.shape[1]
    total = lax.axis_size("ctx") * rows
    scale = 1.0 / math.sqrt(lax.axis_size("dp") * total)
    z = jnp.dot(feats, w_in, preferred_element_type=jnp.float32).astype(jnp.bfloat16)
    before = shifted(z[rows - rim :], "ctx", 1)
    padded = jnp.concatenate([before, z], axis=0)
    mixed = jnp.zeros((rows, z.shape[1]), jnp.float32)
    for j in range(rim + 1):
        mixed = mixed + conv_taps[j] * padded[rim - j : rim - j + rows].astype(jnp.float32)
    query = mixed[:, :width]
    keyed = mixed[:, width : 2 * width]
    valued = mixed[:, 2 * width :]
    product = (keyed * valued).astype(jnp.bfloat16)
    amp_mine = jnp.sqrt(-jnp.expm1(-2.0 * rates))
    reff = residues * amp_mine
    blk = min(BLK, total)
    spread = lax.all_to_all(product.T, "ctx", split_axis=0, concat_axis=1, tiled=True)
    u3 = spread.reshape(spread.shape[0], total // blk, blk)
    empty = jnp.zeros((spread.shape[0], modes), jnp.float32)
    conv3, starts = grouped(forward_local, (u3, reff, rates, empty))
    back = lax.all_to_all(
        conv3.reshape(spread.shape[0], total).astype(jnp.bfloat16),
        "ctx",
        split_axis=1,
        concat_axis=0,
        tiled=True,
    )
    long_out = back.T
    output = (query * long_out.astype(jnp.float32)).astype(jnp.bfloat16)
    upstream = cotangent[0].astype(jnp.float32)
    dquery = upstream * long_out.astype(jnp.float32)
    dlong = (upstream * query).astype(jnp.bfloat16)
    gspread = lax.all_to_all(dlong.T, "ctx", split_axis=0, concat_axis=1, tiled=True)
    g3 = gspread.reshape(gspread.shape[0], total // blk, blk)
    du3, draw = grouped(backward_local, (g3, u3, reff, rates, starts, empty))
    dback = lax.all_to_all(
        du3.reshape(gspread.shape[0], total).astype(jnp.bfloat16),
        "ctx",
        split_axis=1,
        concat_axis=0,
        tiled=True,
    )
    dproduct = dback.T
    filt = draw
    filt = lax.psum(filt, "dp")
    grad_residues = amp_mine * filt * scale
    dprod32 = dproduct.astype(jnp.float32)
    dmixed = jnp.concatenate([dquery, dprod32 * valued, dprod32 * keyed], axis=1).astype(
        jnp.bfloat16
    )
    dm32 = dmixed.astype(jnp.float32)
    tap_rows = []
    for j in range(rim + 1):
        tap_rows.append(
            jnp.sum(dm32 * padded[rim - j : rim - j + rows].astype(jnp.float32), axis=0)
        )
    grad_taps = lax.psum(jnp.stack(tap_rows, axis=0), ("ctx", "dp")) * scale
    after = shifted(dmixed[:rim], "ctx", -1)
    dpad = jnp.concatenate([dmixed, after], axis=0)
    dz = jnp.zeros((rows, dmixed.shape[1]), jnp.float32)
    for j in range(rim + 1):
        dz = dz + conv_taps[j] * dpad[j : j + rows].astype(jnp.float32)
    dz = dz.astype(jnp.bfloat16)
    grad_feats = lax.dot_general(
        dz, w_in, (((1,), (1,)), ((), ())), preferred_element_type=jnp.float32
    ).astype(jnp.bfloat16)
    full_term = lax.dot_general(
        feats, dz, (((0,), (0,)), ((), ())), preferred_element_type=jnp.float32
    )
    feat_count = full_term.shape[0]
    chan_count = full_term.shape[1]
    ctx_count = lax.axis_size("ctx")
    pieces = full_term.reshape(ctx_count, feat_count // ctx_count, chan_count)
    arrived = lax.all_to_all(
        pieces.astype(jnp.bfloat16), "ctx", split_axis=0, concat_axis=0, tiled=True
    ).astype(pieces.dtype)
    row_part = jnp.sum(arrived, axis=0)
    weight_sum = lax.psum_scatter(
        row_part.astype(jnp.bfloat16), "dp", scatter_dimension=1, tiled=True
    ).astype(jnp.float32)
    grad_weight = (weight_sum * scale).astype(jnp.bfloat16)
    return (output[None], grad_feats[None], grad_weight, grad_taps, grad_residues)


def solution(mesh):
    in_specs = (
        P("dp", "ctx", None),
        P(),
        P(),
        P("ctx", None),
        P("ctx", None),
        P("dp", "ctx", None),
    )
    out_specs = (P("dp", "ctx", None), P("dp", "ctx", None), P("ctx", "dp"), P(), P("ctx", None))
    return jax.shard_map(local, mesh=mesh, in_specs=in_specs, out_specs=out_specs, check_vma=False)
```

profile of v0, /device:TPU:0, one launch (start us, length us, event | category | flops | bytes accessed | tf_op | source)
XLA Modules:
  0.0 399.4 jit_solution(16827432109016573585)
XLA Ops:
  8.0 1.0 copy-done
  9.0 6.0 %convolution_convert_fusion.1 = bf16[128,2880]{0,1:T(8,128)(2,1)S(1)} fusion(bf16[1536,2880]{0,1:T(8,128)(2,1)} %param.7, bf16[1,128,1536]{2,1,0:T(8,128)(2,1)S(1)} %copy-done), kind=kOutput, calls=%fused_computation.18 | convolution fusion | flops 1132830720 | bytes 9977856 | tf_op jit(solution)/shard_map/dot_general | solution.py:102
  15.6 2.4 collective-permute-start
  18.0 0.6 fusion.117
  18.6 0.6 multiply_convert_fusion.2
  19.4 0.8 slice_reduce_fusion.6
  20.3 0.6 multiply_reduce_fusion
  21.5 54.4 %gather_fusion = f32[16384,120]{1,0:T(8,128)} fusion(f32[120,128]{0,1:T(8,128)S(1)} %copy.84, s32[16384]{0:T(1024)S(1)} %bitcast_clamp_fusion), kind=kCustom, calls=%fused_computation | custom fusion | bytes 15794176 | tf_op jit(solution)/shard_map/while/body/eval_jaxpr/gather | solution.py:35
  75.9 9.2 %copy.69 = f32[128,128,120]{1,0,2:T(8,128)} copy(f32[128,128,120]{2,1,0:T(8,128)} %bitcast.89) | data formatting | bytes 15728640 | tf_op jit(solution)/shard_map/while/body/eval_jaxpr/gather | solution.py:35
  85.6 6.4 %fusion.14 = f32[128,2880]{0,1:T(8,128)S(1)} fusion(bf16[128,2880]{0,1:T(8,128)(2,1)S(1)} %convolution_convert_fusion.1, f32[2880]{0:T(1024)S(1)} %copy-done.25, f32[2880]{0:T(1024)} %get-tuple-element.70, f32[2880]{0:T(1024)S(1)} %copy-done.17, f32[2880]{0:T(1024)S(1)} %copy-done.19, f32[2880]{0:T(1024)S(1)} %copy-done.21, f32[2880]{0:T(1024)S(1)} %copy-done.23, ...), kind=kLoop, calls=%fused_computation.45 | loop fusion | flops 14008320 | bytes 2327040 | tf_op jit(solution)/shard_map/add | solution.py:107
  92.0 0.7 fusion.61
  92.8 5.0 %all-to-all-start.2 = ((bf16[8,120,128]{2,1,0:T(8,128)(2,1)}), bf16[8,120,128]{2,1,0:T(8,128)(2,1)}, u32[]{:S(2)}, u32[]{:S(2)}) async-start(bf16[8,120,128]{2,1,0:T(8,128)(2,1)} %bitcast.93), calls=%async_computation.2 | async-start | bytes 491520 | tf_op jit(solution)/shard_map/all_to_all | solution.py:131
  98.3 6.3 %all-to-all-done.2 = bf16[8,120,128]{2,1,0:T(8,128)(2,1)} async-done(((bf16[8,120,128]{2,1,0:T(8,128)(2,1)}), bf16[8,120,128]{2,1,0:T(8,128)(2,1)}, u32[]{:S(2)}, u32[]{:S(2)}) %all-to-all-start.2) | async-done | bytes 245792 | tf_op jit(solution)/shard_map/all_to_all | solution.py:131
  104.6 1.4 fusion.52
  106.0 2.2 convolution_add_fusion.2
  108.2 1.8 copy.102
  110.1 1.0 multiply_reduce_fusion.1
  111.1 1.0 copy.97
  112.1 4.5 %fusion.56 = f32[120,8,128]{2,1,0:T(8,128)S(1)} fusion(f32[128,128,120]{1,0,2:T(8,128)} %copy.69, pred[128,128]{1,0:T(8,128)(4,1)S(1)} %subtract_compare_fusion, bf16[8,120,128]{2,1,0:T(8,128)(2,1)} %all-to-all-done.2), kind=kOutput, calls=%fused_computation.96 | convolution fusion | flops 41287680 | bytes 8617984 | tf_op jit(solution)/shard_map/while/body/eval_jaxpr/cbi,cij->cbj/dot_general | solution.py:28
  116.6 4.6 %fusion.36 = f32[120,8,128]{2,1,0:T(8,128)S(1)} fusion(f32[120,8,128]{2,1,0:T(8,128)S(1)} %fusion.56, f32[128,128,120]{1,0,2:T(8,128)} %copy.69, pred[128,128]{1,0:T(8,128)(4,1)S(1)} %subtract_compare_fusion, bf16[8,120,128]{2,1,0:T(8,128)(2,1)} %all-to-all-done.2), kind=kOutput, calls=%fused_computation.66 | convolution fusion | flops 33546240 | bytes 9109504 | tf_op jit(solution)/shard_map/while/body/eval_jaxpr/cbi,cij->cbj/dot_general | solution.py:27
  121.2 0.8 fusion.38
  122.0 0.7 copy.74
  122.7 4.0 %all-to-all-start.3 = ((bf16[120,8,128]{2,0,1:T(8,128)(2,1)}), bf16[120,8,128]{2,0,1:T(8,128)(2,1)}, u32[]{:S(2)}, u32[]{:S(2)}) async-start(bf16[120,8,128]{2,0,1:T(8,128)(2,1)} %copy.74), calls=%async_computation.3 | async-start | bytes 491520 | tf_op jit(solution)/shard_map/all_to_all | solution.py:134
  126.8 6.8 %all-to-all-done.3 = bf16[120,8,128]{2,0,1:T(8,128)(2,1)} async-done(((bf16[120,8,128]{2,0,1:T(8,128)(2,1)}), bf16[120,8,128]{2,0,1:T(8,128)(2,1)}, u32[]{:S(2)}, u32[]{:S(2)}) %all-to-all-start.3) | async-done | bytes 245792 | tf_op jit(solution)/shard_map/all_to_all | solution.py:134
  133.5 1.9 fusion.62
  135.4 4.2 %all-to-all-start = ((bf16[8,120,128]{2,1,0:T(8,128)(2,1)}), bf16[8,120,128]{2,1,0:T(8,128)(2,1)}, u32[]{:S(2)}, u32[]{:S(2)}) async-start(bf16[8,120,128]{2,1,0:T(8,128)(2,1)} %bitcast.92), calls=%async_computation | async-start | bytes 491520 | tf_op jit(solution)/shard_map/all_to_all | solution.py:115
  139.6 0.5 multiply_convert_fusion.4
  140.2 0.5 broadcast_add_fusion
  140.7 5.5 %all-to-all-done = bf16[8,120,128]{2,1,0:T(8,128)(2,1)} async-done(((bf16[8,120,128]{2,1,0:T(8,128)(2,1)}), bf16[8,120,128]{2,1,0:T(8,128)(2,1)}, u32[]{:S(2)}, u32[]{:S(2)}) %all-to-all-start) | async-done | bytes 245792 | tf_op jit(solution)/shard_map/all_to_all | solution.py:115
  146.2 1.4 fusion.54
  147.6 2.2 convolution_add_fusion.3
  149.8 1.2 copy.101
  150.9 1.6 multiply_reduce_fusion.2
  152.6 1.8 copy.91
  154.4 5.5 %fusion.58 = f32[120,8,128]{2,1,0:T(8,128)S(1)} fusion(f32[128,128,120]{1,0,2:T(8,128)} %copy.69, pred[128,128]{1,0:T(8,128)(4,1)S(1)} %subtract_compare_fusion, bf16[8,120,128]{2,1,0:T(8,128)(2,1)} %all-to-all-done), kind=kOutput, calls=%fused_computation.97 | convolution fusion | flops 41287680 | bytes 8617984 | tf_op jit(solution)/shard_map/while/body/eval_jaxpr/cbj,cij->cbi/dot_general | solution.py:28
  159.9 5.6 %fusion.35 = f32[120,8,128]{2,1,0:T(8,128)S(1)} fusion(f32[120,8,128]{2,1,0:T(8,128)S(1)} %fusion.58, f32[128,128,120]{1,0,2:T(8,128)} %copy.69, pred[128,128]{1,0:T(8,128)(4,1)S(1)} %subtract_compare_fusion, bf16[8,120,128]{2,1,0:T(8,128)(2,1)} %all-to-all-done), kind=kOutput, calls=%fused_computation.65 | convolution fusion | flops 33546240 | bytes 9109504 | tf_op jit(solution)/shard_map/while/body/eval_jaxpr/cbj,cij->cbi/dot_general | solution.py:27
  165.5 0.8 fusion.37
  166.4 9.3 %all_to_all.51 = bf16[120,8,128]{2,0,1:T(8,128)(2,1)S(1)} all-to-all(bf16[120,8,128]{2,0,1:T(8,128)(2,1)S(1)} %copy.72), channel_id=1, replica_groups=mesh['ctx'=8,'dp'=4] {'ctx'}, dimensions={1} | all-to-all | bytes 491520 | tf_op jit(solution)/shard_map/all_to_all | solution.py:119
  175.7 0.8 fusion.60
  176.5 0.9 pad_maximum_fusion.2
  177.4 1.4 copy.75
  178.9 1.3 collective-permute-start.1
  180.2 1.8 collective-permute-done.1
  182.0 1.2 copy.76
  183.3 1.4 pad_maximum_fusion
  184.7 1.1 copy-done.9
  185.9 11.3 %fusion = bf16[1536,2880]{0,1:T(8,128)(2,1)} fusion(bf16[1,128,1536]{2,1,0:T(8,128)(2,1)S(1)} %copy-done, bf16[134,2880]{0,1:T(8,128)(2,1)S(1)} %pad_maximum_fusion, f32[2880]{0:T(1024)S(1)} %copy-done.26, f32[2880]{0:T(1024)S(1)} %copy-done.27, f32[2880]{0:T(1024)S(1)} %copy-done.18, f32[2880]{0:T(1024)S(1)} %copy-done.20, f32[2880]{0:T(1024)S(1)} %copy-done.22, ...), kind=kOutput, calls=%fused_computation.2 | convolution fusion | flops 1146470400 | bytes 14487552 | tf_op jit(solution)/shard_map/dot_general | solution.py:165
  197.2 12.5 %copy.77 = bf16[1536,2880]{1,0:T(8,128)(2,1)} copy(bf16[1536,2880]{0,1:T(8,128)(2,1)} %fusion) | data formatting | bytes 17694720 | tf_op jit(solution)/shard_map/convert_element_type | solution.py:173
  209.7 5.0 %all-to-all-start.4 = ((bf16[8,192,2880]{2,1,0:T(8,128)(2,1)}), bf16[8,192,2880]{2,1,0:T(8,128)(2,1)}, u32[]{:S(2)}, u32[]{:S(2)}) async-start(bf16[8,192,2880]{2,1,0:T(8,128)(2,1)} %bitcast.88), calls=%async_computation.4 | async-start | bytes 18087936 | tf_op jit(solution)/shard_map/all_to_all | solution.py:172
  215.1 5.4 %fusion.87 = f32[120,128,128]{2,1,0:T(8,128)} fusion(bf16[8,120,128]{2,1,0:T(8,128)(2,1)} %all-to-all-done.2, bf16[8,120,128]{2,1,0:T(8,128)(2,1)} %all-to-all-done), kind=kOutput, calls=%fused_computation.134 | convolution fusion | flops 31457280 | bytes 8355840 | tf_op jit(solution)/shard_map/while/body/eval_jaxpr/cbi,cbj->cij/dot_general | solution.py:73
  220.5 5.0 %fusion.27 = (f32[2880]{0:T(1024)S(1)}, f32[2880]{0:T(1024)S(1)}, f32[2880]{0:T(1024)S(1)}, f32[2880]{0:T(1024)S(1)}, f32[2880]{0:T(1024)S(1)}, /*index=5*/f32[2880]{0:T(1024)S(1)}, f32[2880]{0:T(1024)S(1)}) fusion(bf16[128,2880]{0,1:T(8,128)(2,1)S(1)} %convolution_convert_fusion.1, bf16[6,2880]{0,1:T(8,128)(2,1)S(1)} %copy.66, ...), kind=kLoop, calls=%fused_computation.58 | loop fusion | flops 16568640 | bytes 1589760 | tf_op jit(solution)/shard_map/reduce_sum | solution.py:153
  225.7 0.8 stack.31
  226.5 1.5 multiply_reduce_fusion.3
  228.0 88.3 %all-to-all-done.4 = bf16[8,192,2880]{2,1,0:T(8,128)(2,1)} async-done(((bf16[8,192,2880]{2,1,0:T(8,128)(2,1)}), bf16[8,192,2880]{2,1,0:T(8,128)(2,1)}, u32[]{:S(2)}, u32[]{:S(2)}) %all-to-all-start.4) | async-done | bytes 8847392 | tf_op jit(solution)/shard_map/all_to_all | solution.py:172
  316.4 5.5 %reduce_sum.95 = bf16[192,2880]{1,0:T(8,128)(2,1)S(1)} reduce(bf16[8,192,2880]{2,1,0:T(8,128)(2,1)} %all-to-all-done.4, bf16[]{:T(256)} %constant.56.clone.1), dimensions={0}, to_apply=%region_0.1 | reduce | flops 3870720 | bytes 9953282 | tf_op jit(solution)/shard_map/reduce_sum | solution.py:175
  321.9 1.7 copy.98
  323.6 8.7 %fusion.32 = f32[120,16]{1,0:T(8,128)S(1)} fusion(f32[120,128,128]{2,1,0:T(8,128)} %fusion.87, pred[128,128]{1,0:T(8,128)(4,1)S(1)} %subtract_compare_fusion, f32[120,16]{1,0:T(8,128)S(1)} %copy.79, f32[128]{0:T(128)S(1)} %copy-done.33, f32[120,16]{1,0:T(8,128)S(1)} %copy.68), kind=kOutput, calls=%fused_computation.62 | convolution fusion | flops 191690880 | bytes 7904256 | tf_op jit(solution)/shard_map/while/body/eval_jaxpr/cij,ckj->cki/dot_general | solution.py:76
  332.4 13.3 %psum.15 = f32[120,16]{0,1:T(8,128)S(1)} all-reduce(f32[120,16]{0,1:T(8,128)S(1)} %multiply_add_fusion.2), channel_id=1, replica_groups=mesh['ctx'=8,'dp'=4] {'dp'}, use_global_device_ids=true, to_apply=%region_12.13 | all-reduce | flops 1920 | bytes 15360 | tf_op jit(solution)/shard_map/psum | solution.py:143
  345.7 0.6 multiply_multiply_fusion
  346.3 14.6 %fusion.8 = bf16[1,128,1536]{2,1,0:T(8,128)(2,1)} fusion(bf16[1536,2880]{0,1:T(8,128)(2,1)} %param.7, bf16[134,2880]{0,1:T(8,128)(2,1)} %copy-done.9, f32[2880]{0:T(1024)S(1)} %copy-done.26, f32[2880]{0:T(1024)S(1)} %copy-done.27, f32[2880]{0:T(1024)S(1)} %copy-done.18, f32[2880]{0:T(1024)S(1)} %copy-done.20, f32[2880]{0:T(1024)S(1)} %copy-done.22, ...), kind=kOutput, calls=%fused_computation.22 | convolution fusion | flops 1142243328 | bytes 14482176 | tf_op jit(solution)/shard_map/dot_general | solution.py:162
  361.0 27.6 %all-reduce.2.cloned.1.call-done = f32[7,2880]{1,0:T(8,128)} async-done(((f32[7,2880]{1,0:T(8,128)}), f32[7,2880]{1,0:T(8,128)}) %all-reduce.2.cloned.1.call-update) | async-done | bytes 80656 | tf_op jit(solution)/shard_map/psum | solution.py:155
  388.5 1.5 broadcast_multiply_fusion
  390.1 1.1 copy.99
  391.2 0.8 multiply_convert_fusion
  (103 shorter events, 3.3 us)
Async XLA Ops:
  8.0 1.0 copy-start
  15.0 4.2 %copy-start.13 = (f32[120,16]{0,1:T(8,128)S(1)}, f32[120,16]{0,1:T(8,128)}, u32[]{:S(2)}) copy-start(f32[120,16]{0,1:T(8,128)} %param.10) | copy-start | bytes 23044
  15.0 4.2 %copy-start.29 = (f32[120,16]{0,1:T(8,128)S(1)}, f32[120,16]{0,1:T(8,128)}, u32[]{:S(2)}) copy-start(f32[120,16]{0,1:T(8,128)} %param.9) | copy-start | bytes 23044
  15.0 4.4 %copy-start.14 = (f32[7,2880]{1,0:T(8,128)S(1)}, f32[7,2880]{1,0:T(8,128)}, u32[]{:S(2)}) copy-start(f32[7,2880]{1,0:T(8,128)} %param.8) | copy-start | bytes 241924
  15.6 69.5 %collective-permute-start = (bf16[6,2880]{1,0:T(8,128)(2,1)S(1)}, bf16[6,2880]{1,0:T(8,128)(2,1)S(1)}, u32[]{:S(2)}, u32[]{:S(2)}) collective-permute-start(bf16[6,2880]{1,0:T(8,128)(2,1)S(1)} %copy.65), channel_id=1, source_target_pairs={{0,4},{4,8},{8,12},{12,16},{16,20},{20,24},{24,28},{1,5},{5,9},{9,... | collective-permute-start | bytes 103688 | tf_op jit(solution)/shard_map/ppermute | solution.py:17
  18.0 57.9 %copy-start.31 = (f32[128]{0:T(128)}, f32[128]{0:T(128)S(1)}, u32[]{:S(2)}) copy-start(f32[128]{0:T(128)S(1)} %iota_convert_fusion) | copy-start | bytes 1540
  19.2 1.6 copy-start.28
  20.3 65.3 %copy-start.15 = (f32[2880]{0:T(1024)}, f32[2880]{0:T(1024)S(1)}, u32[]{:S(2)}) copy-start(f32[2880]{0:T(1024)S(1)} %get-tuple-element.64) | copy-start | bytes 34564
  75.9 9.7 %copy-start.17 = (f32[2880]{0:T(1024)S(1)}, f32[2880]{0:T(1024)}, u32[]{:S(2)}) copy-start(f32[2880]{0:T(1024)} %get-tuple-element.65) | copy-start | bytes 34564
  75.9 9.7 %copy-start.19 = (f32[2880]{0:T(1024)S(1)}, f32[2880]{0:T(1024)}, u32[]{:S(2)}) copy-start(f32[2880]{0:T(1024)} %get-tuple-element.66) | copy-start | bytes 34564
  75.9 9.7 %copy-start.21 = (f32[2880]{0:T(1024)S(1)}, f32[2880]{0:T(1024)}, u32[]{:S(2)}) copy-start(f32[2880]{0:T(1024)} %get-tuple-element.67) | copy-start | bytes 34564
  75.9 9.7 %copy-start.23 = (f32[2880]{0:T(1024)S(1)}, f32[2880]{0:T(1024)}, u32[]{:S(2)}) copy-start(f32[2880]{0:T(1024)} %get-tuple-element.68) | copy-start | bytes 34564
  75.9 9.7 %copy-start.25 = (f32[2880]{0:T(1024)S(1)}, f32[2880]{0:T(1024)}, u32[]{:S(2)}) copy-start(f32[2880]{0:T(1024)} %get-tuple-element.69) | copy-start | bytes 34564
  85.6 6.4 %copy-start.10 = (bf16[1,128,960]{1,2,0:T(8,128)(2,1)S(1)}, bf16[1,128,960]{1,2,0:T(8,128)(2,1)}, u32[]{:S(2)}) copy-start(bf16[1,128,960]{1,2,0:T(8,128)(2,1)} %param.11) | copy-start | bytes 737284
  92.0 12.6 %copy-start.32 = (f32[128]{0:T(128)S(1)}, f32[128]{0:T(128)}, u32[]{:S(2)}) copy-start(f32[128]{0:T(128)} %copy-done.31) | copy-start | bytes 1540
  92.8 11.9 %all-to-all-start.2 = ((bf16[8,120,128]{2,1,0:T(8,128)(2,1)}), bf16[8,120,128]{2,1,0:T(8,128)(2,1)}, u32[]{:S(2)}, u32[]{:S(2)}) async-start(bf16[8,120,128]{2,1,0:T(8,128)(2,1)} %bitcast.93), calls=%async_computation.2 | async-start | bytes 491520 | tf_op jit(solution)/shard_map/all_to_all | solution.py:131
  116.6 4.6 %copy-start.12 = (f32[120,16,8]{1,2,0:T(8,128)S(1)}, f32[120,16,8]{1,2,0:T(8,128)}, u32[]{:S(2)}) copy-start(f32[120,16,8]{1,2,0:T(8,128)} %copy.97) | copy-start | bytes 184324
  116.6 4.6 %copy-start.34 = (f32[128]{0:T(128)S(1)}, f32[128]{0:T(128)}, u32[]{:S(2)}) copy-start(f32[128]{0:T(128)} %broadcast_subtract_fusion) | copy-start | bytes 1540
  116.6 4.6 %copy-start.36 = (f32[8]{0:T(128)S(1)}, f32[8]{0:T(128)}, u32[]{:S(2)}) copy-start(f32[8]{0:T(128)} %multiply_convert_fusion.3) | copy-start | bytes 100
  122.7 10.8 %all-to-all-start.3 = ((bf16[120,8,128]{2,0,1:T(8,128)(2,1)}), bf16[120,8,128]{2,0,1:T(8,128)(2,1)}, u32[]{:S(2)}, u32[]{:S(2)}) async-start(bf16[120,8,128]{2,0,1:T(8,128)(2,1)} %copy.74), calls=%async_computation.3 | async-start | bytes 491520 | tf_op jit(solution)/shard_map/all_to_all | solution.py:134
  135.4 10.8 %all-to-all-start = ((bf16[8,120,128]{2,1,0:T(8,128)(2,1)}), bf16[8,120,128]{2,1,0:T(8,128)(2,1)}, u32[]{:S(2)}, u32[]{:S(2)}) async-start(bf16[8,120,128]{2,1,0:T(8,128)(2,1)} %bitcast.92), calls=%async_computation | async-start | bytes 491520 | tf_op jit(solution)/shard_map/all_to_all | solution.py:115
  159.9 5.6 %copy-start.8 = (f32[120,16,8]{1,2,0:T(8,128)S(1)}, f32[120,16,8]{1,2,0:T(8,128)}, u32[]{:S(2)}) copy-start(f32[120,16,8]{1,2,0:T(8,128)} %copy.91) | copy-start | bytes 184324
  159.9 5.6 %copy-start.30 = (f32[8]{0:T(128)S(1)}, f32[8]{0:T(128)}, u32[]{:S(2)}) copy-start(f32[8]{0:T(128)} %multiply_convert_fusion.4) | copy-start | bytes 100
  159.9 5.6 %copy-start.35 = (f32[128]{0:T(128)S(1)}, f32[128]{0:T(128)}, u32[]{:S(2)}) copy-start(f32[128]{0:T(128)} %broadcast_add_fusion) | copy-start | bytes 1540
  165.5 10.2 %copy-start.11 = (bf16[1,128,960]{1,2,0:T(8,128)(2,1)S(1)}, bf16[1,128,960]{1,2,0:T(8,128)(2,1)}, u32[]{:S(2)}) copy-start(bf16[1,128,960]{1,2,0:T(8,128)(2,1)} %param.11) | copy-start | bytes 737284
  166.3 10.2 %copy-start.2 = (bf16[128,960]{0,1:T(8,128)(2,1)S(1)}, bf16[128,960]{0,1:T(8,128)(2,1)}, u32[]{:S(2)}) copy-start(bf16[128,960]{0,1:T(8,128)(2,1)} %get-tuple-element.75) | copy-start | bytes 737284
  166.3 10.2 %copy-start.4 = (bf16[128,960]{0,1:T(8,128)(2,1)S(1)}, bf16[128,960]{0,1:T(8,128)(2,1)}, u32[]{:S(2)}) copy-start(bf16[128,960]{0,1:T(8,128)(2,1)} %get-tuple-element.76) | copy-start | bytes 737284
  176.5 0.9 copy-start.6
  176.5 6.7 %copy-start.3 = (bf16[128,960]{0,1:T(8,128)(2,1)S(1)}, bf16[128,960]{0,1:T(8,128)(2,1)}, u32[]{:S(2)}) copy-start(bf16[128,960]{0,1:T(8,128)(2,1)} %get-tuple-element.75) | copy-start | bytes 737284
  176.5 6.7 %copy-start.5 = (bf16[128,960]{0,1:T(8,128)(2,1)S(1)}, bf16[128,960]{0,1:T(8,128)(2,1)}, u32[]{:S(2)}) copy-start(bf16[128,960]{0,1:T(8,128)(2,1)} %get-tuple-element.76) | copy-start | bytes 737284
  177.4 5.8 %copy-start.7 = (bf16[128,960]{0,1:T(8,128)(2,1)S(1)}, bf16[128,960]{0,1:T(8,128)(2,1)}, u32[]{:S(2)}) copy-start(bf16[128,960]{0,1:T(8,128)(2,1)} %copy-done.6) | copy-start | bytes 737284
  178.9 3.1 collective-permute-start.1
  183.2 2.6 copy-start.16
  183.2 2.6 copy-start.18
  183.2 2.6 copy-start.20
  183.2 2.6 copy-start.22
  183.2 2.6 copy-start.24
  183.3 2.6 copy-start.26
  183.3 2.6 copy-start.27
  184.7 1.1 copy-start.9
  209.7 106.7 %all-to-all-start.4 = ((bf16[8,192,2880]{2,1,0:T(8,128)(2,1)}), bf16[8,192,2880]{2,1,0:T(8,128)(2,1)}, u32[]{:S(2)}, u32[]{:S(2)}) async-start(bf16[8,192,2880]{2,1,0:T(8,128)(2,1)} %bitcast.88), calls=%async_computation.4 | async-start | bytes 18087936 | tf_op jit(solution)/shard_map/all_to_all | solution.py:172
  214.7 173.8 %all-reduce.2.cloned.1.call-start = ((), (), s32[]{:S(2)}) async-start(), calls=%async_computation.6 | async-start | bytes 188416 | tf_op jit(solution)/shard_map/psum | solution.py:155
  226.5 163.6 %reduce-scatter.4.cloned.1.call-start = ((), (), s32[]{:S(2)}) async-start(), calls=%async_computation.7 | async-start | bytes 1843200
  321.9 1.7 copy-start.33
  346.3 45.6 %copy-start.1 = (bf16[1,128,1536]{2,1,0:T(8,128)(2,1)S(1)}, bf16[1,128,1536]{2,1,0:T(8,128)(2,1)}, u32[]{:S(2)}) copy-start(bf16[1,128,1536]{2,1,0:T(8,128)(2,1)} %param.6) | copy-start | bytes 1179652
Sparse Core Ops, SparseCore 0:
  226.6 161.9 all-reduce.1
Sparse Core Ops, SparseCore 1:
  323.7 34.2 reduce-scatter.3
where the time goes:
time: 401 us; the launch traced here: 399 us
  waiting for transfers between devices  136 us (34%)
  local copies, waits for them, and re-layouts  93.5 us (23%)
  matrix products  74.9 us (19%)
  other arithmetic  33.7 us (8%)
  blocking collectives  22.6 us (6%)
  starting transfers between devices  22.2 us (6%)
  between operations  16.1 us (4%)
    all_to_all x1, waiting for transfers between devices, local(): lax.all_to_all(pieces.astype(jnp.bfloat16), 'ctx', split_axis=0, concat_a...  88.3 us
    gather x2, local copies, waits for them, and re-layouts, lag_matrix(): return jnp.where(index[None] >= 0, lagged[:, jnp.maximum(index, 0)], 0.0)  63.6 us
    psum x1, waiting for transfers between devices, local(): grad_taps = lax.psum(jnp.stack(tap_rows, axis=0), ('ctx', 'dp')) * scale  27.6 us
    dot_general x1, matrix products, local(): lax.dot_general(dz, w_in, (((1,), (1,)), ((), ())), preferred_element_typ...  14.6 us
    dot_general x4, matrix products, mixed_dot(): jnp.einsum(form, data, lower, preferred_element_type=jnp.float32)  14.4 us
    psum x1, blocking collectives, local(): filt = lax.psum(filt, 'dp')  13.3 us
    dot_general x4, matrix products, mixed_dot(): first = jnp.einsum(form, data, upper, preferred_element_type=jnp.float32)  12.9 us
    convert_element_type x1, local copies, waits for them, and re-layouts, local(): pieces.astype(jnp.bfloat16)  12.5 us
  transfers between devices with their start and end apart: 8, of which 6 were waited for; matrix products, arithmetic and copies ran while one was open for 29% of the time, Pallas kernels for 0%

commit v1 on v0

v1 whole, which is shorter than its diff:
```python
import functools
import math

import jax
import jax.numpy as jnp
from jax import lax
from jax.experimental import pallas as pl
from jax.experimental.pallas import tpu as pltpu
from jax.sharding import PartitionSpec as P

LANES = 128
SUB = 8
HALO = 16
GROUP = 32

VM = pl.BlockSpec(memory_space=pltpu.VMEM)
SM = pl.BlockSpec(memory_space=pltpu.SMEM)
PARAMS = pltpu.CompilerParams(vmem_limit_bytes=48 << 20)
f32 = jnp.float32
bf16 = jnp.bfloat16


def lane_tiles(width):
    return [(a, min(a + LANES, width)) for a in range(0, width, LANES)]


def sub_index(first, sign, lanes):
    rows = lax.broadcasted_iota(jnp.int32, (SUB, lanes), 0).astype(f32)
    return first + sign * rows


def fold_down(rate, load, blocks, first, sign, order):
    ratio = jnp.exp(-float(SUB) * rate)
    total = None
    for a in order(blocks):
        block = load(a)
        total = block if total is None else total * ratio + block
    weight = jnp.exp(-rate * sub_index(first, sign, rate.shape[1]))
    return jnp.sum(total * weight, axis=0, keepdims=True)


def forwards(blocks):
    return list(range(blocks))


def backwards(blocks):
    return list(range(blocks - 1, -1, -1))


def states_kernel(width, z_ref, taps_ref, cot_ref, rate_ref, qkv_ref, up_ref, gp_ref, eh_ref, zs, mixed):
    rows = cot_ref.shape[0]
    count = taps_ref.shape[0]
    modes, wide = rate_ref.shape
    blocks = rows // SUB
    for a, b in lane_tiles(z_ref.shape[1]):
        zs[:, a:b] = z_ref[:, a:b].astype(f32)
        total = jnp.zeros((rows, b - a), f32)
        for j in range(count):
            total = total + taps_ref[j : j + 1, a:b] * zs[HALO - j : HALO - j + rows, a:b]
        mixed[:, a:b] = total
    if wide > width:
        for part in range(3):
            qkv_ref[part, :, width:] = jnp.zeros((rows, wide - width), f32)
        up_ref[:, width:] = jnp.zeros((2 * rows, wide - width), f32)
        gp_ref[:, width:] = jnp.zeros((2 * rows, wide - width), f32)
    up_ref[:rows, :width] = jnp.zeros((rows, width), f32)
    gp_ref[rows:, :width] = jnp.zeros((rows, width), f32)
    for part in range(3):
        qkv_ref[part, :, :width] = mixed[:, part * width : (part + 1) * width]
    for a, b in lane_tiles(width):
        product = (qkv_ref[1, :, a:b] * qkv_ref[2, :, a:b]).astype(bf16)
        up_ref[rows:, a:b] = product.astype(f32)
        dlong = (cot_ref[:, a:b].astype(f32) * qkv_ref[0, :, a:b]).astype(bf16)
        gp_ref[:rows, a:b] = dlong.astype(f32)
    for a, b in lane_tiles(wide):
        for k in range(modes):
            rate = rate_ref[k : k + 1, a:b]
            eh_ref[k : k + 1, a:b] = fold_down(
                rate, lambda i: up_ref[rows + i * SUB : rows + (i + 1) * SUB, a:b],
                blocks, float(SUB - 1), -1.0, forwards)
            eh_ref[modes + k : modes + k + 1, a:b] = fold_down(
                rate, lambda i: gp_ref[i * SUB : (i + 1) * SUB, a:b], blocks, 0.0, 1.0, backwards)


def spread_modes(rate_ref, coef, ref, lanes, first, sign, order, blocks):
    modes = rate_ref.shape[0]
    totals = [ref[i * SUB : (i + 1) * SUB, lanes] for i in range(blocks)]
    for k in range(modes):
        rate = rate_ref[k : k + 1, lanes]
        ratio = jnp.exp(-float(SUB) * rate)
        term = coef(k) * jnp.exp(-rate * sub_index(first, sign, LANES))
        steps = order(blocks)
        for i in steps:
            totals[i] = totals[i] + term
            if i != steps[-1]:
                term = term * ratio
    for i in range(blocks):
        ref[i * SUB : (i + 1) * SUB, lanes] = totals[i]


def near_kernel(up_ref, gp_ref, rate_ref, reff_ref, inf_ref, inb_ref, near_ref, filt, corr, ups, gps):
    rows = inf_ref.shape[0]
    modes, wide = rate_ref.shape
    blocks = rows // SUB
    inf_ref[...] = jnp.zeros((rows, wide), f32)
    inb_ref[...] = jnp.zeros((rows, wide), f32)
    filt[...] = jnp.zeros((rows, wide), f32)
    index = lax.broadcasted_iota(jnp.int32, (SUB, LANES), 0)

    @pl.loop(0, wide // LANES)
    def _(tile):
        lanes = pl.ds(pl.multiple_of(tile * LANES, LANES), LANES)
        spread_modes(rate_ref, lambda k: reff_ref[k : k + 1, lanes], filt, lanes, 0.0, 1.0, forwards, blocks)
        for s in range(SUB):
            ups[s, SUB:, :] = up_ref[SUB - s : 2 * rows - s, lanes]
            gps[s, : 2 * rows - SUB, :] = gp_ref[s : 2 * rows - SUB + s, lanes]
        for low in range(0, rows, GROUP):
            size = rows - low

            def body(step, carry):
                acc_f, acc_b = carry
                base = pl.multiple_of(low + step * SUB, SUB)
                taps = filt[pl.ds(base, SUB), lanes]
                lags = jnp.zeros((SUB, LANES), f32)
                for s in range(SUB):
                    tap = taps[s : s + 1]
                    moved = ups[s, pl.ds(pl.multiple_of(rows + low - base, SUB), size), :]
                    acc_f = acc_f + tap * moved
                    pair = jnp.sum(gp_ref[low:rows, lanes] * moved, axis=0, keepdims=True)
                    lags = jnp.where(index == s, pair, lags)
                    acc_b = acc_b + tap * gps[s, pl.ds(base, size), :]
                corr[pl.ds(base, SUB), lanes] = lags
                return acc_f, acc_b

            acc_f, acc_b = lax.fori_loop(
                0, GROUP // SUB, body, (inf_ref[low:rows, lanes], inb_ref[0:size, lanes]))
            inf_ref[low:rows, lanes] = acc_f
            inb_ref[0:size, lanes] = acc_b
        for k in range(modes):
            near_ref[k : k + 1, lanes] = fold_down(
                rate_ref[k : k + 1, lanes], lambda i: corr[i * SUB : (i + 1) * SUB, lanes],
                blocks, 0.0, 1.0, backwards)


def join_kernel(width, me_ref, qkv_ref, inf_ref, inb_ref, near_ref, cot_ref, rate_ref, reff_ref, all_ref, z_ref,
                out_ref, dm_ref, tap_ref, draw_ref, first, last, lf, lb, dm, zs):
    rows = cot_ref.shape[0]
    modes, wide = rate_ref.shape
    blocks = rows // SUB
    devices = all_ref.shape[0]
    count = tap_ref.shape[0]
    me = me_ref[0]
    rate = rate_ref[...]
    first[...] = jnp.zeros((modes, wide), f32)
    last[...] = jnp.zeros((modes, wide), f32)

    @pl.loop(0, devices)
    def _(d):
        ahead = jnp.maximum(me - 1 - d, 0).astype(f32)
        keep = jnp.where(d < me, 1.0, 0.0)
        first[...] += keep * jnp.exp(-rate * (ahead * float(rows))) * all_ref[d, 0:modes]
        behind = jnp.maximum(d - me - 1, 0).astype(f32)
        hold = jnp.where(d > me, 1.0, 0.0)
        last[...] += hold * jnp.exp(-rate * (behind * float(rows))) * all_ref[d, modes : 2 * modes]

    draw_ref[...] = near_ref[...] + first[...] * all_ref[me, modes : 2 * modes] * jnp.exp(-rate)
    first[...] = first[...] * reff_ref[...]
    last[...] = last[...] * reff_ref[...]
    lf[...] = inf_ref[...]
    lb[...] = inb_ref[...]

    @pl.loop(0, wide // LANES)
    def _(tile):
        lanes = pl.ds(pl.multiple_of(tile * LANES, LANES), LANES)
        spread_modes(rate_ref, lambda k: first[k : k + 1, lanes], lf, lanes, 1.0, 1.0, forwards, blocks)
        spread_modes(rate_ref, lambda k: last[k : k + 1, lanes], lb, lanes, float(SUB), -1.0, backwards, blocks)

    for a, b in lane_tiles(width):
        far = lf[:, a:b].astype(bf16).astype(f32)
        out_ref[:, a:b] = (qkv_ref[0, :, a:b] * far).astype(bf16)
        lf[:, a:b] = cot_ref[:, a:b].astype(f32) * far
        lb[:, a:b] = lb[:, a:b].astype(bf16).astype(f32)
    dm[:, 0:width] = lf[:, 0:width]
    dm[:, width : 2 * width] = lb[:, 0:width] * qkv_ref[2, :, 0:width]
    dm[:, 2 * width : 3 * width] = lb[:, 0:width] * qkv_ref[1, :, 0:width]
    for a, b in lane_tiles(3 * width):
        held = dm[:, a:b].astype(bf16)
        dm_ref[:, a:b] = held
        held = held.astype(f32)
        zs[:, a:b] = z_ref[:, a:b].astype(f32)
        for j in range(count):
            tap_ref[j : j + 1, a:b] = jnp.sum(
                held * zs[HALO - j : HALO - j + rows, a:b], axis=0, keepdims=True)


def dz_kernel(dm_ref, after_ref, taps_ref, dz_ref, cut_ref, pad, full):
    rows = dm_ref.shape[0]
    parts, _, piece = cut_ref.shape
    count = taps_ref.shape[0]
    for a, b in lane_tiles(dm_ref.shape[1]):
        pad[0:rows, a:b] = dm_ref[:, a:b].astype(f32)
        pad[rows:, a:b] = after_ref[:, a:b].astype(f32)
        total = jnp.zeros((rows, b - a), f32)
        for j in range(count):
            total = total + taps_ref[j : j + 1, a:b] * pad[j : j + rows, a:b]
        dz_ref[:, a:b] = total.astype(bf16)
        full[:, a:b] = total
    for p in range(parts):
        cut_ref[p] = full[:, p * piece : (p + 1) * piece].astype(bf16)


def shape(dims, kind=f32):
    return jax.ShapeDtypeStruct(dims, kind)


def call(kernel, outs, scratch, ops, scalars=0, flops=10**8):
    return pl.pallas_call(
        kernel,
        out_shape=outs,
        in_specs=[SM] * scalars + [VM] * (len(ops) - scalars),
        out_specs=[VM] * len(outs),
        scratch_shapes=[pltpu.VMEM(dims, f32) for dims in scratch],
        compiler_params=PARAMS,
        cost_estimate=pl.CostEstimate(flops=flops, bytes_accessed=1 << 22, transcendentals=0),
    )(*ops)


def shifted(block, axis, distance):
    devices = range(lax.axis_size(axis))
    route = [(i - distance, i) for i in devices if i - distance in devices]
    return lax.ppermute(block, axis, route)


def local(tokens, w_in, conv_taps, residues, rates, cotangent):
    feats = tokens[0]
    rows, depth = feats.shape
    cot = cotangent[0]
    width = cot.shape[1]
    chans = w_in.shape[1]
    own, modes = rates.shape
    count = conv_taps.shape[0]
    ctx = lax.axis_size("ctx")
    dp = lax.axis_size("dp")
    me = lax.axis_index("ctx")
    scale = 1.0 / math.sqrt(dp * ctx * rows)
    wide = -(-width // LANES) * LANES

    amp = jnp.sqrt(-jnp.expm1(-2.0 * rates))
    modal = jnp.concatenate([rates.T, (residues * amp).T], axis=0)
    modal = lax.all_gather(modal, "ctx", axis=0, tiled=False)
    modal = modal.transpose(1, 0, 2).reshape(2 * modes, width)
    modal = jnp.pad(modal, ((0, 0), (0, wide - width)))
    rate_t, reff_t = modal[:modes], modal[modes:]

    before = shifted(feats[rows - HALO :], "ctx", 1)
    stacked = jnp.concatenate([before, feats], axis=0)
    z = jnp.dot(stacked, w_in, preferred_element_type=f32).astype(bf16)

    qkv, up, gp, eh = call(
        functools.partial(states_kernel, width),
        [shape((3, rows, wide)), shape((2 * rows, wide)), shape((2 * rows, wide)), shape((2 * modes, wide))],
        [(HALO + rows, chans), (rows, chans)],
        (z, conv_taps, cot, rate_t))
    every = lax.all_gather(eh, "ctx", axis=0, tiled=False)
    inner_f, inner_b, near = call(
        near_kernel,
        [shape((rows, wide)), shape((rows, wide)), shape((modes, wide))],
        [(rows, wide), (rows, wide), (SUB, 2 * rows, LANES), (SUB, 2 * rows, LANES)],
        (up, gp, rate_t, reff_t), flops=5 * 10**9)
    output, dmixed, tap_part, draw = call(
        functools.partial(join_kernel, width),
        [shape((rows, width), bf16), shape((rows, chans), bf16), shape((count, chans)), shape((modes, wide))],
        [(modes, wide), (modes, wide), (rows, wide), (rows, wide), (rows, chans), (HALO + rows, chans)],
        (me.reshape(1), qkv, inner_f, inner_b, near, cot, rate_t, reff_t, every, z), scalars=1)

    after = shifted(dmixed[:HALO], "ctx", -1)
    dz, cut = call(
        dz_kernel,
        [shape((rows, chans), bf16), shape((dp, rows, chans // dp), bf16)],
        [(rows + HALO, chans), (rows, chans)],
        (dmixed, after, conv_taps))

    feats_all = lax.all_gather(feats, "dp", axis=0, tiled=True)
    swapped = lax.all_to_all(cut, "dp", split_axis=0, concat_axis=0, tiled=True)
    grad_feats = lax.dot_general(
        dz, w_in, (((1,), (1,)), ((), ())), preferred_element_type=f32).astype(bf16)
    term = lax.dot_general(
        feats_all, swapped.reshape(dp * rows, chans // dp), (((0,), (0,)), ((), ())),
        preferred_element_type=f32).astype(bf16)
    arrived = lax.all_to_all(
        term.reshape(ctx, depth // ctx, chans // dp), "ctx", split_axis=0, concat_axis=0, tiled=True)
    grad_weight = (jnp.sum(arrived.astype(f32), axis=0) * scale).astype(bf16)

    tap_sum, draw_sum = lax.psum((tap_part, draw[:, :width]), ("ctx", "dp"))
    grad_taps = tap_sum * scale
    mine = lax.dynamic_slice_in_dim(draw_sum, me * own, own, axis=1)
    grad_residues = amp * mine.T * scale
    return (output[None], grad_feats[None], grad_weight, grad_taps, grad_residues)


def solution(mesh):
    in_specs = (
        P("dp", "ctx", None),
        P(),
        P(),
        P("ctx", None),
        P("ctx", None),
        P("dp", "ctx", None),
    )
    out_specs = (P("dp", "ctx", None), P("dp", "ctx", None), P("ctx", "dp"), P(), P("ctx", None))
    return jax.shard_map(local, mesh=mesh, in_specs=in_specs, out_specs=out_specs, check_vma=False)
```

time: 401 us -> 270 us (0.67)
  local copies, waits for them, and re-layouts: 93.5 us -> 14 us
  matrix products: 74.9 us -> 15.3 us
  blocking collectives: 22.6 us -> 70.8 us
  other arithmetic: 33.7 us -> 4.75 us
  Pallas kernels: 0 us -> 25 us
  waiting for transfers between devices: 136 us -> 113 us
  starting transfers between devices: 22.2 us -> 12.4 us
    all_to_all x4 -> x2, waiting for transfers between devices: 107 us -> 0.01 us  [the longest x1 0.01 us: local(): lax.all_to_all(term.reshape(ctx, depth // ctx, chans // dp), 'ctx', split...]
    gather x2 -> x0, local copies, waits for them, and re-layouts: 63.6 us -> none  [lag_matrix(): return jnp.where(index[None] >= 0, lagged[:, jnp.maximum(index, 0)], 0.0)]
    dot_general x14 -> x2, matrix products: 60.3 us -> 9.67 us  [the longest x1 6.73 us: local(): z = jnp.dot(stacked, w_in, preferred_element_type=f32).astype(bf16)]
    psum x1, blocking collectives: 13.3 us -> 60.5 us  [local(): tap_sum, draw_sum = lax.psum((tap_part, draw[:, :width]), ('ctx', 'dp'))]
    all_gather x0 -> x2, waiting for transfers between devices: none -> 41.9 us  [the longest x1 36.6 us: local(): feats_all = lax.all_gather(feats, 'dp', axis=0, tiled=True)]
    psum x1, waiting for transfers between devices: 27.6 us -> 68 us  [local(): tap_sum, draw_sum = lax.psum((tap_part, draw[:, :width]), ('ctx', 'dp'))]
    pallas_call x0 -> x4, Pallas kernels: none -> 25 us  [call(): pl.pallas_call(kernel, out_shape=outs, in_specs=[SM] * scalars + [VM] * (...]
    reduce_sum x3 -> x1, other arithmetic: 12 us -> 0.35 us  [local(): grad_weight = (jnp.sum(arrived.astype(f32), axis=0) * scale).astype(bf16)]
  transfers between devices with their start and end apart: 8 -> 7, of which waited for: 6 -> 4; matrix products, arithmetic and copies ran while one was open for 29% -> 5% of each run, Pallas kernels for 0% -> 8%
where the time goes in v1:
time: 270 us; the launch traced here: 269 us
  waiting for transfers between devices  113 us (42%)
  blocking collectives  70.8 us (26%)
  Pallas kernels  25 us (9%)
  matrix products  15.3 us (6%)
  local copies, waits for them, and re-layouts  14 us (5%)
  between operations  13.9 us (5%)
  starting transfers between devices  12.4 us (5%)
  other arithmetic  4.75 us (2%)
    psum x1, waiting for transfers between devices, local(): tap_sum, draw_sum = lax.psum((tap_part, draw[:, :width]), ('ctx', 'dp'))  68 us
    psum x1, blocking collectives, local(): tap_sum, draw_sum = lax.psum((tap_part, draw[:, :width]), ('ctx', 'dp'))  60.5 us
    all_gather x1, waiting for transfers between devices, local(): feats_all = lax.all_gather(feats, 'dp', axis=0, tiled=True)  36.6 us
    pallas_call x4, Pallas kernels, call(): pl.pallas_call(kernel, out_shape=outs, in_specs=[SM] * scalars + [VM] * (...  25 us
    all_gather x1, blocking collectives, local(): modal = lax.all_gather(modal, 'ctx', axis=0, tiled=False)  10.3 us
    unnamed x28, local copies, waits for them, and re-layouts  9.42 us
    dot_general x1, matrix products, local(): z = jnp.dot(stacked, w_in, preferred_element_type=f32).astype(bf16)  6.73 us
    dot_general x1, matrix products, local(): lax.dot_general(dz, w_in, (((1,), (1,)), ((), ())), preferred_element_typ...  5.68 us
  transfers between devices with their start and end apart: 7, of which 4 were waited for; matrix products, arithmetic and copies ran while one was open for 5% of the time, Pallas kernels for 8%

profile of v1, /device:TPU:0, one launch (start us, length us, event | category | flops | bytes accessed | tf_op | source)
XLA Modules:
  0.0 269.4 jit_solution(10039429024761093936)
XLA Ops:
  7.2 0.0 all-gather.6.cloned.1.call-start
  7.2 0.8 slice_bitcast_fusion
  8.0 2.3 collective-permute-start
  10.4 0.7 multiply_bitcast_fusion
  11.1 0.7 pad_maximum_fusion
  11.8 10.3 %all-gather = f32[256,120]{1,0:T(8,128)S(1)} all-gather(f32[32,120]{1,0:T(8,128)S(1)} %pad_maximum_fusion), channel_id=2, replica_groups=mesh['ctx'=8,'dp'=4] {'ctx'}, dimensions={0}, use_global_device_ids=true | all-gather | bytes 138240 | tf_op jit(solution)/shard_map/all_gather | solution.py:250
  22.1 0.1 copy.35
  22.2 0.1 reshape.24
  22.3 1.1 copy.23
  23.4 0.0 collective-permute-done
  23.4 0.0 copy-start.3
  23.4 6.7 %convolution_convert_fusion.z_ref = bf16[144,2880]{1,0:T(8,128)(2,1)S(1)} fusion(bf16[1536,2880]{0,1:T(8,128)(2,1)} %param.7, bf16[128,1536]{1,0:T(8,128)(2,1)} %bitcast.43, bf16[16,1536]{1,0:T(8,128)(2,1)S(1)} %collective-permute-done), kind=kOutput, calls=%fused_computation.1 | convolution fusion | flops 1275319296 | bytes 10119168 | tf_op jit(solution)/shard_map/dot_general | solution.py:257
  30.1 0.0 copy-done.3
  30.1 3.9 %shard_map.101 = (f32[3,128,1024]{2,1,0:T(8,128)S(1)}, f32[256,1024]{1,0:T(8,128)S(1)}, f32[256,1024]{1,0:T(8,128)S(1)}, f32[32,1024]{1,0:T(8,128)}) custom-call(bf16[144,2880]{1,0:T(8,128)(2,1)S(1)} %convolution_convert_fusion.z_ref, f32[7,2880]{1,0:T(8,128)S(1)} %copy-done.3, bf16[128,960]{1,0:T(8,128)(2,1)S(1)} %bitcast.37, ...), custom_call_target="tpu_custom_call" | custom-call | flops 100000000 | bytes 4194304 | tf_op jit(solution)/shard_map/pallas_call | solution.py:217
  34.1 0.0 copy-start.8
  34.1 1.0 copy-done.8
  35.1 0.0 copy-start.10
  35.1 1.0 copy-done.10
  36.0 0.0 all-gather.6.cloned.1.call-update
  36.1 0.0 all-gather.8.cloned.1.call-start
  36.1 0.7 all-gather.8.cloned.1.call-update
  36.8 0.0 copy-start.9
  36.8 1.2 copy-done.9
  38.1 0.0 copy-start.11
  38.1 1.2 copy-done.11
  39.3 14.6 %shard_map.102 = (f32[128,1024]{1,0:T(8,128)S(1)}, f32[128,1024]{1,0:T(8,128)S(1)}, f32[16,1024]{1,0:T(8,128)S(1)}) custom-call(f32[256,1024]{1,0:T(8,128)S(1)} %copy-done.9, f32[256,1024]{1,0:T(8,128)S(1)} %copy-done.11, f32[16,1024]{1,0:T(8,128)S(1)} %get-tuple-element.52.rate_ref, f32[16,1024]{1,0:T(8,128)S(1)} %get-tuple-element.51.reff_ref), custom_call_target="tpu_custom_call" | custom-call | flops 5000000000 | bytes 4194304 | tf_op jit(solution)/shard_map/pallas_call | solution.py:217
  53.9 0.0 copy-start.1
  53.9 0.8 copy-done.1
  54.7 5.4 %all-gather.6.cloned.1.call-done = f32[256,1024]{1,0:T(8,128)} async-done(((f32[32,1024]{1,0:T(8,128)}), f32[256,1024]{1,0:T(8,128)}) %all-gather.6.cloned.1.call-update) | async-done | bytes 1048592 | tf_op jit(solution)/shard_map/all_gather | solution.py:264
  60.1 0.0 copy-start
  60.1 1.2 copy-done
  61.3 0.0 copy-start.2
  61.3 1.0 copy-done.2
  62.3 4.6 %shard_map.103 = (bf16[128,960]{1,0:T(8,128)(2,1)S(1)}, bf16[128,2880]{1,0:T(8,128)(2,1)S(1)}, f32[7,2880]{1,0:T(8,128)}, f32[16,1024]{1,0:T(8,128)S(1)}) custom-call(s32[1]{0:T(128)} %bitcast.me_ref, f32[3,128,1024]{2,1,0:T(8,128)S(1)} %get-tuple-element.18.qkv_ref, f32[128,1024]{1,0:T(8,128)S(1)} %get-tuple-element.21.inf_ref, f32[128,1024]{1,0:T(8,128)S(1)} %copy-done.2, ...), custom_call_target="tpu_custom_call" | custom-call | flops 100000000 | bytes 4194304 | tf_op jit(solution)/shard_map/pallas_call | solution.py:217
  66.9 0.0 copy-start.4
  66.9 0.0 copy-start.6
  66.9 1.3 collective-permute-start.1
  68.2 1.9 collective-permute-done.1.after_ref
  70.1 1.8 shard_map.104
  72.0 0.0 copy-done.4
  72.0 0.0 copy-done.6
  72.0 1.1 copy.25
  73.1 4.6 %all-to-all-start = ((bf16[4,128,720]{1,2,0:T(8,128)(2,1)}), bf16[4,128,720]{1,2,0:T(8,128)(2,1)}, u32[]{:S(2)}, u32[]{:S(2)}) async-start(bf16[4,128,720]{1,2,0:T(8,128)(2,1)} %copy.25), calls=%async_computation | async-start | bytes 1474560 | tf_op jit(solution)/shard_map/all_to_all | solution.py:284
  77.7 36.6 %all-gather.8.cloned.1.call-done = bf16[1,512,1536]{2,1,0:T(8,128)(2,1)} async-done(((bf16[1,128,1536]{2,1,0:T(8,128)(2,1)}), bf16[1,512,1536]{2,1,0:T(8,128)(2,1)}) %all-gather.8.cloned.1.call-update) | async-done | bytes 1572880 | tf_op jit(solution)/shard_map/all_gather | solution.py:283
  114.3 0.0 all-to-all-done
  114.3 2.9 %fusion = bf16[1536,720]{0,1:T(8,128)(2,1)S(1)} fusion(bf16[1,512,1536]{2,1,0:T(8,128)(2,1)} %all-gather.8.cloned.1.call-done, bf16[4,128,720]{1,2,0:T(8,128)(2,1)} %all-to-all-done), kind=kOutput, calls=%fused_computation.3 | convolution fusion | flops 1133568000 | bytes 4521984 | tf_op jit(solution)/shard_map/dot_general | solution.py:287
  117.2 2.4 copy.27
  119.7 0.0 copy-start.7
  119.7 0.0 copy-start.12
  119.7 4.1 %all-to-all-start.1 = ((bf16[8,192,720]{2,1,0:T(8,128)(2,1)}), bf16[8,192,720]{2,1,0:T(8,128)(2,1)S(1)}, u32[]{:S(2)}, u32[]{:S(2)}) async-start(bf16[8,192,720]{2,1,0:T(8,128)(2,1)} %bitcast.42), calls=%async_computation.1 | async-start | bytes 4718592 | tf_op jit(solution)/shard_map/all_to_all | solution.py:290
  123.8 0.0 all-reduce.3.cloned.1.call-start
  123.8 0.7 all-reduce.3.cloned.1.call-update
  124.5 0.0 copy-done.7
  124.5 60.5 %psum.15 = f32[16,960]{1,0:T(8,128)S(1)} all-reduce(f32[16,960]{1,0:T(8,128)S(1)} %bitcast.41), channel_id=1, replica_groups=mesh['ctx'=8,'dp'=4] {'ctx','dp'}, use_global_device_ids=true, to_apply=%region_2.3 | all-reduce | flops 15360 | bytes 122880 | tf_op jit(solution)/shard_map/psum | solution.py:294
  185.0 0.0 copy-done.12
  185.0 0.7 fusion.8
  185.7 0.0 copy-done.5
  185.7 0.8 copy.28
  186.6 68.0 %all-reduce.3.cloned.1.call-done = f32[7,2880]{1,0:T(8,128)} async-done(((f32[7,2880]{1,0:T(8,128)}), f32[7,2880]{1,0:T(8,128)}) %all-reduce.3.cloned.1.call-update) | async-done | bytes 80656 | tf_op jit(solution)/shard_map/psum | solution.py:294
  254.6 1.5 broadcast_multiply_fusion
  256.1 5.7 %fusion.1 = bf16[1,128,1536]{2,1,0:T(8,128)(2,1)} fusion(bf16[128,2880]{1,0:T(8,128)(2,1)S(1)} %get-tuple-element.27, bf16[1536,2880]{0,1:T(8,128)(2,1)} %param.7), kind=kOutput, calls=%fused_computation.5 | convolution fusion | flops 1132658688 | bytes 9977856 | tf_op jit(solution)/shard_map/dot_general | solution.py:285
  261.8 0.0 all-to-all-done.1
  261.8 0.3 convert_reduce_fusion
  262.1 0.7 multiply_convert_fusion
  (3 shorter events, 0.0 us)
Async XLA Ops:
  7.2 52.9 %all-gather.6.cloned.1.call-start = ((), (), s32[]{:S(2)}) async-start(), calls=%async_computation.3 | async-start | bytes 1179648 | tf_op jit(solution)/shard_map/all_gather | solution.py:264
  8.0 15.4 %collective-permute-start = (bf16[16,1536]{1,0:T(8,128)(2,1)S(1)}, bf16[16,1536]{1,0:T(8,128)(2,1)S(1)}, u32[]{:S(2)}, u32[]{:S(2)}) collective-permute-start(bf16[16,1536]{1,0:T(8,128)(2,1)S(1)} %slice_bitcast_fusion), channel_id=1, source_target_pairs={{0,4},{4,8},{8,12},{12,16},{16,20},{20,24},{24,28},{1,5},{5,9},{9,... | collective-permute-start | bytes 147464 | tf_op jit(solution)/shard_map/ppermute | solution.py:231
  23.4 6.7 %copy-start.3 = (f32[7,2880]{1,0:T(8,128)S(1)}, f32[7,2880]{1,0:T(8,128)}, u32[]{:S(2)}) copy-start(f32[7,2880]{1,0:T(8,128)} %taps_ref.3) | copy-start | bytes 241924
  34.1 1.0 copy-start.8
  35.1 1.0 copy-start.10
  36.1 78.2 %all-gather.8.cloned.1.call-start = ((), (), s32[]{:S(2)}) async-start(), calls=%async_computation.4 | async-start | bytes 1966080 | tf_op jit(solution)/shard_map/all_gather | solution.py:283
  36.8 1.2 copy-start.9
  38.1 1.2 copy-start.11
  53.9 0.8 copy-start.1
  60.1 1.2 copy-start
  61.3 1.0 copy-start.2
  66.9 5.0 %copy-start.4 = (bf16[128,960]{1,0:T(8,128)(2,1)}, bf16[128,960]{1,0:T(8,128)(2,1)S(1)}, u32[]{:S(2)}) copy-start(bf16[128,960]{1,0:T(8,128)(2,1)S(1)} %get-tuple-element.25) | copy-start | bytes 737284
  66.9 5.0 %copy-start.6 = (f32[16,1024]{1,0:T(8,128)}, f32[16,1024]{1,0:T(8,128)S(1)}, u32[]{:S(2)}) copy-start(f32[16,1024]{1,0:T(8,128)S(1)} %get-tuple-element.30) | copy-start | bytes 196612
  66.9 3.2 %collective-permute-start.1 = (bf16[16,2880]{1,0:T(8,128)(2,1)S(1)}, bf16[16,2880]{1,0:T(8,128)(2,1)S(1)}, u32[]{:S(2)}, u32[]{:S(2)}) collective-permute-start(bf16[16,2880]{1,0:T(8,128)(2,1)S(1)} %slice.22), channel_id=1, source_target_pairs={{4,0},{8,4},{12,8},{16,12},{20,16},{24,20},{28,24},{5,1},{9,5},{13... | collective-permute-start | bytes 276488 | tf_op jit(solution)/shard_map/ppermute | solution.py:231
  73.1 41.2 %all-to-all-start = ((bf16[4,128,720]{1,2,0:T(8,128)(2,1)}), bf16[4,128,720]{1,2,0:T(8,128)(2,1)}, u32[]{:S(2)}, u32[]{:S(2)}) async-start(bf16[4,128,720]{1,2,0:T(8,128)(2,1)} %copy.25), calls=%async_computation | async-start | bytes 1474560 | tf_op jit(solution)/shard_map/all_to_all | solution.py:284
  119.7 4.8 %copy-start.7 = (f32[16,1024]{1,0:T(8,128)S(1)}, f32[16,1024]{1,0:T(8,128)}, u32[]{:S(2)}) copy-start(f32[16,1024]{1,0:T(8,128)} %copy-done.6) | copy-start | bytes 196612
  119.7 65.4 %copy-start.12 = (f32[120,16]{0,1:T(8,128)S(1)}, f32[120,16]{0,1:T(8,128)}, u32[]{:S(2)}) copy-start(f32[120,16]{0,1:T(8,128)} %param.10) | copy-start | bytes 23044
  119.7 66.0 %copy-start.5 = (bf16[128,960]{1,0:T(8,128)(2,1)S(1)}, bf16[128,960]{1,0:T(8,128)(2,1)}, u32[]{:S(2)}) copy-start(bf16[128,960]{1,0:T(8,128)(2,1)} %copy-done.4) | copy-start | bytes 737284
  119.7 142.1 %all-to-all-start.1 = ((bf16[8,192,720]{2,1,0:T(8,128)(2,1)}), bf16[8,192,720]{2,1,0:T(8,128)(2,1)S(1)}, u32[]{:S(2)}, u32[]{:S(2)}) async-start(bf16[8,192,720]{2,1,0:T(8,128)(2,1)} %bitcast.42), calls=%async_computation.1 | async-start | bytes 4718592 | tf_op jit(solution)/shard_map/all_to_all | solution.py:290
  123.8 130.8 %all-reduce.3.cloned.1.call-start = ((), (), s32[]{:S(2)}) async-start(), calls=%async_computation.2 | async-start | bytes 188416 | tf_op jit(solution)/shard_map/psum | solution.py:294
Sparse Core Ops, SparseCore 0:
  36.2 23.8 all-gather.5
  61.6 52.6 all-gather.7
  130.7 123.7 all-reduce.2

commit v2 on v1

--- a/solution.py
+++ b/solution.py
@@ -143,12 +143,12 @@
 
 
 def join_kernel(width, me_ref, qkv_ref, inf_ref, inb_ref, near_ref, cot_ref, rate_ref, reff_ref, all_ref, z_ref,
-                out_ref, dm_ref, tap_ref, draw_ref, first, last, lf, lb, dm, zs):
+                out_ref, dm_ref, stat_ref, first, last, lf, lb, dm, zs, tap_ref, draw_ref):
     rows = cot_ref.shape[0]
     modes, wide = rate_ref.shape
     blocks = rows // SUB
     devices = all_ref.shape[0]
-    count = tap_ref.shape[0]
+    count = tap_ref.shape[0] - 1
     me = me_ref[0]
     rate = rate_ref[...]
     first[...] = jnp.zeros((modes, wide), f32)
@@ -191,6 +191,12 @@
         for j in range(count):
             tap_ref[j : j + 1, a:b] = jnp.sum(
                 held * zs[HALO - j : HALO - j + rows, a:b], axis=0, keepdims=True)
+    stat_ref[...] = jnp.zeros(stat_ref.shape, f32)
+    cols = 3 * width // devices
+    own = width // devices
+    for d in range(devices):
+        stat_ref[d, 0:count, :] = tap_ref[0:count, d * cols : (d + 1) * cols]
+        stat_ref[d, SUB : SUB + modes, 0:own] = draw_ref[:, d * own : (d + 1) * own]
 
 
 def dz_kernel(dm_ref, after_ref, taps_ref, dz_ref, cut_ref, pad, full):
@@ -209,6 +215,166 @@
         cut_ref[p] = full[:, p * piece : (p + 1) * piece].astype(bf16)
 
 
+def others(axis):
+    size = lax.axis_size(axis)
+    me = lax.axis_index(axis)
+    return [lax.rem(me + j, size) for j in range(1, size)]
+
+
+def greet(axes):
+    barrier = pltpu.get_barrier_semaphore()
+    count = 0
+    for axis in axes:
+        for peer in others(axis):
+            pl.semaphore_signal(barrier, inc=1, device_id={axis: peer}, device_id_type=pl.DeviceIdType.MESH)
+            count += 1
+    pl.semaphore_wait(barrier, count)
+
+
+def push(axis, peer, src, dst, send, recv):
+    return pltpu.make_async_remote_copy(
+        src_ref=src, dst_ref=dst, send_sem=send.at[peer], recv_sem=recv.at[lax.axis_index(axis)],
+        device_id={axis: peer}, device_id_type=pl.DeviceIdType.MESH)
+
+
+def arrival(axis, peer, src, dst, send, recv):
+    return pltpu.make_async_remote_copy(
+        src_ref=src, dst_ref=dst, send_sem=send.at[peer], recv_sem=recv.at[peer],
+        device_id={axis: peer}, device_id_type=pl.DeviceIdType.MESH)
+
+
+def start_kernel(feats_ref, modal_ref, halo_ref, all_ref, send, recv, hop_send, hop_recv):
+    me = lax.axis_index("ctx")
+    size = lax.axis_size("ctx")
+    rows = feats_ref.shape[0]
+    greet(["ctx"])
+    hop = pltpu.make_async_remote_copy(
+        src_ref=feats_ref.at[pl.ds(rows - HALO, HALO)], dst_ref=halo_ref, send_sem=hop_send, recv_sem=hop_recv,
+        device_id={"ctx": lax.rem(me + 1, size)}, device_id_type=pl.DeviceIdType.MESH)
+    hop.start()
+    sent = [push("ctx", p, modal_ref, all_ref.at[me], send, recv) for p in others("ctx")]
+    for copy in sent:
+        copy.start()
+    all_ref[me] = modal_ref[...]
+    hop.wait()
+
+    @pl.when(me == 0)
+    def _():
+        halo_ref[...] = jnp.zeros(halo_ref.shape, halo_ref.dtype)
+
+    for p in others("ctx"):
+        arrival("ctx", p, modal_ref, all_ref.at[p], send, recv).wait_recv()
+    for copy in sent:
+        copy.wait_send()
+
+
+def inner_kernel(up_ref, gp_ref, rate_ref, reff_ref, eh_ref, turned_ref, inf_ref, inb_ref, near_ref, all_ref, toks_ref,
+                 filt, corr, ups, gps, send, recv, tok_send, tok_recv):
+    me = lax.axis_index("ctx")
+    mine = lax.axis_index("dp")
+    rows = turned_ref.shape[1]
+
+    def slot(p):
+        return toks_ref.at[:, pl.ds(pl.multiple_of(p * rows, rows), rows)]
+
+    greet(["ctx", "dp"])
+    sent = [push("ctx", p, eh_ref, all_ref.at[me], send, recv) for p in others("ctx")]
+    for copy in sent:
+        copy.start()
+    swaps = [push("dp", p, turned_ref, slot(mine), tok_send, tok_recv) for p in others("dp")]
+    for copy in swaps:
+        copy.start()
+    all_ref[me] = eh_ref[...]
+    toks_ref[:, pl.ds(pl.multiple_of(mine * rows, rows), rows)] = turned_ref[...]
+    near_kernel(up_ref, gp_ref, rate_ref, reff_ref, inf_ref, inb_ref, near_ref, filt, corr, ups, gps)
+    for p in others("ctx"):
+        arrival("ctx", p, eh_ref, all_ref.at[p], send, recv).wait_recv()
+    for p in others("dp"):
+        arrival("dp", p, turned_ref, slot(p), tok_send, tok_recv).wait_recv()
+    for copy in sent + swaps:
+        copy.wait_send()
+
+
+def tokens_kernel(dz_ref, cut_ref, stat_ref, w_ref, got_ref, feats_ref, red_ref,
+                  w_held, parts, column, rest, w_sem, cut_send, cut_recv, st_send, st_recv, col_send, col_recv):
+    me = lax.axis_index("ctx")
+    mine = lax.axis_index("dp")
+    load = pltpu.make_async_copy(w_ref, w_held, w_sem)
+    load.start()
+    greet(["ctx", "dp"])
+    sent = [push("ctx", p, stat_ref.at[p], parts.at[me], st_send, st_recv) for p in others("ctx")]
+    for copy in sent:
+        copy.start()
+    swaps = [push("dp", p, cut_ref.at[p], got_ref.at[mine], cut_send, cut_recv) for p in others("dp")]
+    for copy in swaps:
+        copy.start()
+    got_ref[mine] = cut_ref[mine]
+    total = stat_ref[me]
+    for p in others("ctx"):
+        arrival("ctx", p, stat_ref.at[p], parts.at[p], st_send, st_recv).wait_recv()
+        total = total + parts[p]
+    column[...] = total
+    spread = [push("dp", p, column, rest.at[mine], col_send, col_recv) for p in others("dp")]
+    for copy in spread:
+        copy.start()
+    load.wait()
+    tile = 2 * LANES
+
+    @pl.loop(0, w_held.shape[0] // tile)
+    def _(i):
+        at = pl.ds(pl.multiple_of(i * tile, tile), tile)
+        feats_ref[:, at] = lax.dot_general(
+            dz_ref[...], w_held[at, :], (((1,), (1,)), ((), ())), preferred_element_type=f32).astype(bf16)
+
+    rest[mine] = column[...]
+    for p in others("dp"):
+        arrival("dp", p, column, rest.at[p], col_send, col_recv).wait_recv()
+    total = rest[0]
+    for p in range(1, rest.shape[0]):
+        total = total + rest[p]
+    red_ref[...] = total
+    for p in others("dp"):
+        arrival("dp", p, cut_ref.at[p], got_ref.at[p], cut_send, cut_recv).wait_recv()
+    for copy in sent + swaps + spread:
+        copy.wait_send()
+
+
+def weight_kernel(scale, toks_ref, got_ref, red_ref, gw_ref, taps_ref, term, land, total, send, recv, tap_send, tap_recv):
+    me = lax.axis_index("ctx")
+    devices, own, _ = term.shape
+    per = 16 // math.gcd(own, 16)
+    count = devices // per
+    greet(["ctx"])
+    sent = [push("ctx", p, red_ref, taps_ref.at[me], tap_send, tap_recv) for p in others("ctx")]
+    for copy in sent:
+        copy.start()
+    taps_ref[me] = red_ref[...]
+
+    @pl.loop(0, count)
+    def _(i):
+        block = lax.rem(me // per + 1 + i, count)
+        at = pl.ds(pl.multiple_of(block * (own * per), 16), own * per)
+        piece = jnp.dot(toks_ref[at, :], got_ref[...], preferred_element_type=f32)
+        for s in range(per):
+            target = block * per + s
+            term[target] = piece[s * own : (s + 1) * own].astype(bf16)
+
+            @pl.when(target != me)
+            def _():
+                push("ctx", target, term.at[target], land.at[me], send, recv).start()
+
+    total[...] = term[me].astype(f32)
+    for p in others("ctx"):
+        arrival("ctx", p, term.at[p], land.at[p], send, recv).wait_recv()
+        total[...] += land[p].astype(f32)
+    gw_ref[...] = (total[...] * scale).astype(bf16)
+    for p in others("ctx"):
+        arrival("ctx", p, red_ref, taps_ref.at[p], tap_send, tap_recv).wait_recv()
+        arrival("ctx", p, term.at[p], land.at[p], send, recv).wait_send()
+    for copy in sent:
+        copy.wait_send()
+
+
 def shape(dims, kind=f32):
     return jax.ShapeDtypeStruct(dims, kind)
 
@@ -221,6 +387,20 @@
         out_specs=[VM] * len(outs),
         scratch_shapes=[pltpu.VMEM(dims, f32) for dims in scratch],
         compiler_params=PARAMS,
+        cost_estimate=pl.CostEstimate(flops=flops, bytes_accessed=1 << 22, transcendentals=0),
+    )(*ops)
+
+
+def exchange(kernel, number, outs, scratch, ops, anywhere=(), flops=10**8):
+    specs = [pl.BlockSpec(memory_space=pl.ANY) if i in anywhere else VM for i in range(len(ops))]
+    return pl.pallas_call(
+        kernel,
+        out_shape=outs,
+        in_specs=specs,
+        out_specs=[VM] * len(outs),
+        scratch_shapes=scratch,
+        compiler_params=pltpu.CompilerParams(
+            vmem_limit_bytes=48 << 20, collective_id=number, has_side_effects=True),
         cost_estimate=pl.CostEstimate(flops=flops, bytes_accessed=1 << 22, transcendentals=0),
     )(*ops)
 
@@ -246,13 +426,17 @@
     wide = -(-width // LANES) * LANES
 
     amp = jnp.sqrt(-jnp.expm1(-2.0 * rates))
+    dma = pltpu.SemaphoreType.DMA
     modal = jnp.concatenate([rates.T, (residues * amp).T], axis=0)
-    modal = lax.all_gather(modal, "ctx", axis=0, tiled=False)
+    before, modal = exchange(
+        start_kernel, 0,
+        [shape((HALO, depth), bf16), shape((ctx, 2 * modes, own))],
+        [dma((ctx,)), dma((ctx,)), dma, dma],
+        (feats, modal))
     modal = modal.transpose(1, 0, 2).reshape(2 * modes, width)
     modal = jnp.pad(modal, ((0, 0), (0, wide - width)))
     rate_t, reff_t = modal[:modes], modal[modes:]
 
-    before = shifted(feats[rows - HALO :], "ctx", 1)
     stacked = jnp.concatenate([before, feats], axis=0)
     z = jnp.dot(stacked, w_in, preferred_element_type=f32).astype(bf16)
 
@@ -261,16 +445,20 @@
         [shape((3, rows, wide)), shape((2 * rows, wide)), shape((2 * rows, wide)), shape((2 * modes, wide))],
         [(HALO + rows, chans), (rows, chans)],
         (z, conv_taps, cot, rate_t))
-    every = lax.all_gather(eh, "ctx", axis=0, tiled=False)
-    inner_f, inner_b, near = call(
-        near_kernel,
-        [shape((rows, wide)), shape((rows, wide)), shape((modes, wide))],
-        [(rows, wide), (rows, wide), (SUB, 2 * rows, LANES), (SUB, 2 * rows, LANES)],
-        (up, gp, rate_t, reff_t), flops=5 * 10**9)
-    output, dmixed, tap_part, draw = call(
+    inner_f, inner_b, near, every, toks = exchange(
+        inner_kernel, 1,
+        [shape((rows, wide)), shape((rows, wide)), shape((modes, wide)), shape((ctx, 2 * modes, wide)),
+         shape((depth, dp * rows), bf16)],
+        [pltpu.VMEM((rows, wide), f32), pltpu.VMEM((rows, wide), f32),
+         pltpu.VMEM((SUB, 2 * rows, LANES), f32), pltpu.VMEM((SUB, 2 * rows, LANES), f32),
+         dma((ctx,)), dma((ctx,)), dma((dp,)), dma((dp,))],
+        (up, gp, rate_t, reff_t, eh, feats.T), flops=5 * 10**9)
+    output, dmixed, stat = call(
         functools.partial(join_kernel, width),
-        [shape((rows, width), bf16), shape((rows, chans), bf16), shape((count, chans)), shape((modes, wide))],
-        [(modes, wide), (modes, wide), (rows, wide), (rows, wide), (rows, chans), (HALO + rows, chans)],
+        [shape((rows, width), bf16), shape((rows, chans), bf16),
+         shape((ctx, SUB + modes, chans // ctx))],
+        [(modes, wide), (modes, wide), (rows, wide), (rows, wide), (rows, chans), (HALO + rows, chans),
+         (count + 1, chans), (modes, wide)],
         (me.reshape(1), qkv, inner_f, inner_b, near, cot, rate_t, reff_t, every, z), scalars=1)
 
     after = shifted(dmixed[:HALO], "ctx", -1)
@@ -280,21 +468,23 @@
         [(rows + HALO, chans), (rows, chans)],
         (dmixed, after, conv_taps))
 
-    feats_all = lax.all_gather(feats, "dp", axis=0, tiled=True)
-    swapped = lax.all_to_all(cut, "dp", split_axis=0, concat_axis=0, tiled=True)
-    grad_feats = lax.dot_general(
-        dz, w_in, (((1,), (1,)), ((), ())), preferred_element_type=f32).astype(bf16)
-    term = lax.dot_general(
-        feats_all, swapped.reshape(dp * rows, chans // dp), (((0,), (0,)), ((), ())),
-        preferred_element_type=f32).astype(bf16)
-    arrived = lax.all_to_all(
-        term.reshape(ctx, depth // ctx, chans // dp), "ctx", split_axis=0, concat_axis=0, tiled=True)
-    grad_weight = (jnp.sum(arrived.astype(f32), axis=0) * scale).astype(bf16)
-
-    tap_sum, draw_sum = lax.psum((tap_part, draw[:, :width]), ("ctx", "dp"))
-    grad_taps = tap_sum * scale
-    mine = lax.dynamic_slice_in_dim(draw_sum, me * own, own, axis=1)
-    grad_residues = amp * mine.T * scale
+    piece = chans // dp
+    own_feats = depth // ctx
+    unit = (SUB + modes, chans // ctx)
+    got, grad_feats, red = exchange(
+        tokens_kernel, 2,
+        [shape((dp, rows, piece), bf16), shape((rows, depth), bf16), shape(unit)],
+        [pltpu.VMEM((depth, chans), bf16), pltpu.VMEM((ctx,) + unit, f32), pltpu.VMEM(unit, f32),
+         pltpu.VMEM((dp,) + unit, f32), dma, dma((dp,)), dma((dp,)), dma((ctx,)), dma((ctx,)), dma((dp,)), dma((dp,))],
+        (dz, cut, stat, w_in), anywhere=(3,))
+    grad_weight, taps = exchange(
+        functools.partial(weight_kernel, scale), 3,
+        [shape((own_feats, piece), bf16), shape((ctx,) + unit)],
+        [pltpu.VMEM((ctx, own_feats, piece), bf16), pltpu.VMEM((ctx, own_feats, piece), bf16),
+         pltpu.VMEM((own_feats, piece), f32), dma((ctx,)), dma((ctx,)), dma((ctx,)), dma((ctx,))],
+        (toks, got.reshape(dp * rows, piece), red))
+    grad_taps = taps[:, :count].transpose(1, 0, 2).reshape(count, chans) * scale
+    grad_residues = amp * red[SUB:, :own].T * scale
     return (output[None], grad_feats[None], grad_weight, grad_taps, grad_residues)
 
 

time: 270 us -> 146 us (0.54)
  waiting for transfers between devices: 113 us -> 0.01 us
  Pallas kernels: 25 us -> 114 us
  blocking collectives: 70.8 us -> 0 us
  between operations: 13.9 us -> 0.82 us
  starting transfers between devices: 12.4 us -> 1.47 us
  matrix products: 15.3 us -> 6.43 us
  local copies, waits for them, and re-layouts: 14 us -> 19.5 us
    pallas_call x0 -> x4, Pallas kernels: none -> 104 us  [exchange(): pl.pallas_call(kernel, out_shape=outs, in_specs=specs, out_specs=[VM] * l...]
    psum x1 -> x0, waiting for transfers between devices: 68 us -> none  [local(): tap_sum, draw_sum = lax.psum((tap_part, draw[:, :width]), ('ctx', 'dp'))]
    psum x1 -> x0, blocking collectives: 60.5 us -> none  [local(): tap_sum, draw_sum = lax.psum((tap_part, draw[:, :width]), ('ctx', 'dp'))]
    all_gather x2 -> x0, waiting for transfers between devices: 41.9 us -> none  [the longest x1 36.6 us: local(): feats_all = lax.all_gather(feats, 'dp', axis=0, tiled=True)]
    pallas_call x4 -> x3, Pallas kernels: 25 us -> 10.5 us  [call(): pl.pallas_call(kernel, out_shape=outs, in_specs=[SM] * scalars + [VM] * (...]
    all_gather x1 -> x0, blocking collectives: 10.3 us -> none  [local(): modal = lax.all_gather(modal, 'ctx', axis=0, tiled=False)]
    unnamed x28 -> x18, local copies, waits for them, and re-layouts: 9.42 us -> 18.3 us
    all_to_all x2 -> x0, starting transfers between devices: 8.66 us -> none  [the longest x1 4.6 us: local(): swapped = lax.all_to_all(cut, 'dp', split_axis=0, concat_axis=0, tiled=True)]
  transfers between devices with their start and end apart: 7 -> 1, of which waited for: 4 -> 0; matrix products, arithmetic and copies ran while one was open for 5% -> 9% of each run, Pallas kernels for 8% -> 0%
where the time goes in v2:
time: 146 us; the launch traced here: 144 us
  Pallas kernels  114 us (78%)
  local copies, waits for them, and re-layouts  19.5 us (13%)
  matrix products  6.43 us (4%)
  other arithmetic  2.07 us (1%)
  starting transfers between devices  1.47 us (1%)
    pallas_call x4, Pallas kernels, exchange(): pl.pallas_call(kernel, out_shape=outs, in_specs=specs, out_specs=[VM] * l...  104 us
    unnamed x18, local copies, waits for them, and re-layouts  18.3 us
    pallas_call x3, Pallas kernels, call(): pl.pallas_call(kernel, out_shape=outs, in_specs=[SM] * scalars + [VM] * (...  10.5 us
    dot_general x1, matrix products, local(): z = jnp.dot(stacked, w_in, preferred_element_type=f32).astype(bf16)  6.43 us
  transfers between devices with their start and end apart: 1, of which 0 were waited for; matrix products, arithmetic and copies ran while one was open for 9% of the time, Pallas kernels for 0%

profile of v2, /device:TPU:0, one launch (start us, length us, event | category | flops | bytes accessed | tf_op | source)
XLA Modules:
  0.0 144.4 jit_solution(10977243793788420497)
XLA Ops:
  0.6 0.0 copy-start.4
  0.6 1.3 copy.18
  1.9 0.7 multiply_bitcast_fusion.1
  2.6 0.7 pad_maximum_fusion.modal_ref
  3.4 0.0 copy-start.1
  3.4 1.0 copy-done.1
  4.3 7.3 %shard_map.101 = (bf16[16,1536]{1,0:T(8,128)(2,1)S(1)}, f32[8,32,120]{2,1,0:T(8,128)S(1)}) custom-call(bf16[128,1536]{1,0:T(8,128)(2,1)S(1)} %bitcast.24, f32[32,120]{1,0:T(8,128)S(1)} %pad_maximum_fusion.modal_ref), custom_call_target="tpu_custom_call" | custom-call | flops 100000000 | bytes 4194304 | tf_op jit(solution)/shard_map/pallas_call | solution.py:396
  11.6 0.1 copy.22
  11.7 0.1 reshape.23
  11.8 0.0 copy-done.4
  11.8 0.1 copy.21
  12.0 0.2 copy.20
  12.2 0.0 copy-start.3
  12.2 6.4 %convolution_convert_fusion.z_ref = bf16[144,2880]{1,0:T(8,128)(2,1)S(1)} fusion(bf16[1536,2880]{0,1:T(8,128)(2,1)} %param.7, bf16[128,1536]{0,1:T(8,128)(2,1)S(1)} %bitcast.22, bf16[16,1536]{0,1:T(8,128)(2,1)S(1)} %copy.20), kind=kOutput, calls=%fused_computation | convolution fusion | flops 1275319296 | bytes 10119168 | tf_op jit(solution)/shard_map/dot_general | solution.py:441
  18.7 0.0 copy-done.3
  18.7 3.3 %shard_map.102 = (f32[3,128,1024]{2,1,0:T(8,128)S(1)}, f32[256,1024]{1,0:T(8,128)S(1)}, f32[256,1024]{1,0:T(8,128)S(1)}, f32[32,1024]{1,0:T(8,128)S(1)}) custom-call(bf16[144,2880]{1,0:T(8,128)(2,1)S(1)} %convolution_convert_fusion.z_ref, f32[7,2880]{1,0:T(8,128)S(1)} %copy-done.3, bf16[128,960]{1,0:T(8,128)(2,1)S(1)} %bitcast.20, ...), custom_call_target="tpu_custom_call" | custom-call | flops 100000000 | bytes 4194304 | tf_op jit(solution)/shard_map/pallas_call | solution.py:383
  22.0 0.0 copy-start.2
  22.0 1.2 copy-done.2
  23.2 33.1 %shard_map.103 = (f32[128,1024]{1,0:T(8,128)S(1)}, f32[128,1024]{1,0:T(8,128)S(1)}, f32[16,1024]{1,0:T(8,128)S(1)}, f32[8,32,1024]{2,1,0:T(8,128)S(1)}, bf16[1536,512]{1,0:T(8,128)(2,1)}) custom-call(f32[256,1024]{1,0:T(8,128)S(1)} %get-tuple-element.29.up_ref, f32[256,1024]{1,0:T(8,128)S(1)} %get-tuple-element.30.gp_ref, ...), custom_call_target="tpu_custom_call" | custom-call | flops 5000000000 | bytes 4194304 | tf_op jit(solution)/shard_map/pallas_call | solution.py:396
  56.3 5.4 %shard_map.104 = (bf16[128,960]{1,0:T(8,128)(2,1)S(1)}, bf16[128,2880]{1,0:T(8,128)(2,1)S(1)}, f32[8,24,360]{2,1,0:T(8,128)S(1)}) custom-call(s32[1]{0:T(128)} %bitcast.me_ref, f32[3,128,1024]{2,1,0:T(8,128)} %copy-done.2, f32[128,1024]{1,0:T(8,128)S(1)} %get-tuple-element.32.inf_ref, f32[128,1024]{1,0:T(8,128)S(1)} %get-tuple-element.33.inb_ref, ...), custom_call_target="tpu_custom_call" | custom-call | flops 100000000 | bytes 4194304 | tf_op jit(solution)/shard_map/pallas_call | solution.py:383
  61.7 1.5 %collective-permute-start = (bf16[16,2880]{1,0:T(8,128)(2,1)S(1)}, bf16[16,2880]{1,0:T(8,128)(2,1)S(1)}, u32[]{:S(2)}, u32[]{:S(2)}) collective-permute-start(bf16[16,2880]{1,0:T(8,128)(2,1)S(1)} %slice.17), channel_id=1, source_target_pairs={{4,0},{8,4},{12,8},{16,12},{20,16},{24,20},{28,24},{5,1},{9,5},{13... | collective-permute-start | bytes 276488 | tf_op jit(solution)/shard_map/ppermute | solution.py:411
  63.2 12.5 %copy.23.w_ref = bf16[1536,2880]{1,0:T(8,128)(2,1)} copy(bf16[1536,2880]{0,1:T(8,128)(2,1)} %param.7) | data formatting | bytes 17694720 | tf_op args[1]
  75.6 0.8 copy.25
  76.5 0.0 collective-permute-done.after_ref
  76.5 1.8 %shard_map.105 = (bf16[128,2880]{1,0:T(8,128)(2,1)S(1)}, bf16[4,128,720]{2,1,0:T(8,128)(2,1)S(1)}) custom-call(bf16[128,2880]{1,0:T(8,128)(2,1)S(1)} %get-tuple-element.37.dm_ref, bf16[16,2880]{1,0:T(8,128)(2,1)S(1)} %collective-permute-done.after_ref, f32[7,2880]{1,0:T(8,128)S(1)} %copy-done.3), custom_call_target="tpu_custom_call" | custom-call | flops 100000000 | bytes 4194304 | tf_op jit(solution)/shard_map/pallas_call | solution.py:383
  78.3 0.0 copy-start.5
  78.3 0.0 copy-start
  78.3 31.1 %shard_map.106 = (bf16[4,128,720]{2,1,0:T(8,128)(2,1)S(1)}, bf16[128,1536]{1,0:T(8,128)(2,1)S(1)}, f32[24,360]{1,0:T(8,128)S(1)}) custom-call(bf16[128,2880]{1,0:T(8,128)(2,1)S(1)} %get-tuple-element.38.dz_ref, bf16[4,128,720]{2,1,0:T(8,128)(2,1)S(1)} %get-tuple-element.39.cut_ref, f32[8,24,360]{2,1,0:T(8,128)S(1)} %get-tuple-element.40.stat_ref, ...), custom_call_target="tpu_custom_call" | custom-call | flops 100000000 | bytes 4194304 | tf_op jit(solution)/shard_map/pallas_call | solution.py:396
  109.4 0.0 copy-done.5
  109.5 0.6 fusion.3
  110.1 0.0 copy-done
  110.1 32.1 %shard_map.107 = (bf16[192,720]{1,0:T(8,128)(2,1)S(1)}, f32[8,24,360]{2,1,0:T(8,128)S(1)}) custom-call(bf16[1536,512]{1,0:T(8,128)(2,1)S(1)} %copy-done, bf16[512,720]{1,0:T(8,128)(2,1)S(1)} %bitcast.25, f32[24,360]{1,0:T(8,128)S(1)} %get-tuple-element.44.red_ref), custom_call_target="tpu_custom_call" | custom-call | flops 100000000 | bytes 4194304 | tf_op jit(solution)/shard_map/pallas_call | solution.py:396
  142.2 0.7 mul.36
  142.9 0.7 copy.29
  143.7 0.7 copy.30
  (4 shorter events, 0.0 us)
Async XLA Ops:
  0.6 11.2 %copy-start.4 = (bf16[1,128,960]{1,2,0:T(8,128)(2,1)S(1)}, bf16[1,128,960]{1,2,0:T(8,128)(2,1)}, u32[]{:S(2)}) copy-start(bf16[1,128,960]{1,2,0:T(8,128)(2,1)} %param.11) | copy-start | bytes 737284
  3.4 1.0 copy-start.1
  12.2 6.5 %copy-start.3 = (f32[7,2880]{1,0:T(8,128)S(1)}, f32[7,2880]{1,0:T(8,128)}, u32[]{:S(2)}) copy-start(f32[7,2880]{1,0:T(8,128)} %taps_ref.3) | copy-start | bytes 241924
  22.0 1.2 copy-start.2
  61.7 14.8 %collective-permute-start = (bf16[16,2880]{1,0:T(8,128)(2,1)S(1)}, bf16[16,2880]{1,0:T(8,128)(2,1)S(1)}, u32[]{:S(2)}, u32[]{:S(2)}) collective-permute-start(bf16[16,2880]{1,0:T(8,128)(2,1)S(1)} %slice.17), channel_id=1, source_target_pairs={{4,0},{8,4},{12,8},{16,12},{20,16},{24,20},{28,24},{5,1},{9,5},{13... | collective-permute-start | bytes 276488 | tf_op jit(solution)/shard_map/ppermute | solution.py:411
  78.3 31.1 %copy-start.5 = (f32[120,16]{0,1:T(8,128)S(1)}, f32[120,16]{0,1:T(8,128)}, u32[]{:S(2)}) copy-start(f32[120,16]{0,1:T(8,128)} %param.10) | copy-start | bytes 23044
  78.3 31.8 %copy-start = (bf16[1536,512]{1,0:T(8,128)(2,1)S(1)}, bf16[1536,512]{1,0:T(8,128)(2,1)}, u32[]{:S(2)}) copy-start(bf16[1536,512]{1,0:T(8,128)(2,1)} %get-tuple-element.42.toks_ref) | copy-start | bytes 4718596

commit v3 on v2

--- a/solution.py
+++ b/solution.py
@@ -268,47 +268,51 @@
         copy.wait_send()
 
 
-def inner_kernel(up_ref, gp_ref, rate_ref, reff_ref, eh_ref, turned_ref, inf_ref, inb_ref, near_ref, all_ref, toks_ref,
-                 filt, corr, ups, gps, send, recv, tok_send, tok_recv):
+def inner_kernel(up_ref, gp_ref, rate_ref, reff_ref, eh_ref, inf_ref, inb_ref, near_ref, all_ref,
+                 filt, corr, ups, gps, send, recv):
     me = lax.axis_index("ctx")
-    mine = lax.axis_index("dp")
-    rows = turned_ref.shape[1]
-
-    def slot(p):
-        return toks_ref.at[:, pl.ds(pl.multiple_of(p * rows, rows), rows)]
-
-    greet(["ctx", "dp"])
+    greet(["ctx"])
     sent = [push("ctx", p, eh_ref, all_ref.at[me], send, recv) for p in others("ctx")]
     for copy in sent:
-        copy.start()
-    swaps = [push("dp", p, turned_ref, slot(mine), tok_send, tok_recv) for p in others("dp")]
-    for copy in swaps:
         copy.start()
     all_ref[me] = eh_ref[...]
-    toks_ref[:, pl.ds(pl.multiple_of(mine * rows, rows), rows)] = turned_ref[...]
     near_kernel(up_ref, gp_ref, rate_ref, reff_ref, inf_ref, inb_ref, near_ref, filt, corr, ups, gps)
     for p in others("ctx"):
         arrival("ctx", p, eh_ref, all_ref.at[p], send, recv).wait_recv()
-    for p in others("dp"):
-        arrival("dp", p, turned_ref, slot(p), tok_send, tok_recv).wait_recv()
-    for copy in sent + swaps:
+    for copy in sent:
         copy.wait_send()
 
 
-def tokens_kernel(dz_ref, cut_ref, stat_ref, w_ref, got_ref, feats_ref, red_ref,
-                  w_held, parts, column, rest, w_sem, cut_send, cut_recv, st_send, st_recv, col_send, col_recv):
+def tokens_kernel(dm_ref, taps_ref, stat_ref, w_ref, got_ref, feats_ref, red_ref,
+                  w_held, after, dz, cut, pad, full, parts, column, rest, w_sem, hop_send, hop_recv,
+                  cut_send, cut_recv, st_send, st_recv, col_send, col_recv):
     me = lax.axis_index("ctx")
+    size = lax.axis_size("ctx")
     mine = lax.axis_index("dp")
     load = pltpu.make_async_copy(w_ref, w_held, w_sem)
     load.start()
     greet(["ctx", "dp"])
+    hop = pltpu.make_async_remote_copy(
+        src_ref=dm_ref.at[pl.ds(0, HALO)], dst_ref=after, send_sem=hop_send, recv_sem=hop_recv,
+        device_id={"ctx": lax.rem(me + size - 1, size)}, device_id_type=pl.DeviceIdType.MESH)
+    hop.start()
     sent = [push("ctx", p, stat_ref.at[p], parts.at[me], st_send, st_recv) for p in others("ctx")]
     for copy in sent:
         copy.start()
-    swaps = [push("dp", p, cut_ref.at[p], got_ref.at[mine], cut_send, cut_recv) for p in others("dp")]
-    for copy in swaps:
-        copy.start()
-    got_ref[mine] = cut_ref[mine]
+    hop.wait()
+
+    @pl.when(me == size - 1)
+    def _():
+        after[...] = jnp.zeros(after.shape, bf16)
+
+    dz_kernel(dm_ref, after, taps_ref, dz, cut, pad, full)
+    swaps = []
+    for j, p in enumerate(others("dp")):
+        swaps.append(pltpu.make_async_remote_copy(
+            src_ref=cut.at[p], dst_ref=got_ref.at[j + 1], send_sem=cut_send.at[j], recv_sem=cut_recv.at[j],
+            device_id={"dp": p}, device_id_type=pl.DeviceIdType.MESH))
+        swaps[-1].start()
+    got_ref[0] = cut[mine]
     total = stat_ref[me]
     for p in others("ctx"):
         arrival("ctx", p, stat_ref.at[p], parts.at[p], st_send, st_recv).wait_recv()
@@ -320,11 +324,10 @@
     load.wait()
     tile = 2 * LANES
 
-    @pl.loop(0, w_held.shape[0] // tile)
+    @pl.loop(0, w_held.shape[1] // tile)
     def _(i):
         at = pl.ds(pl.multiple_of(i * tile, tile), tile)
-        feats_ref[:, at] = lax.dot_general(
-            dz_ref[...], w_held[at, :], (((1,), (1,)), ((), ())), preferred_element_type=f32).astype(bf16)
+        feats_ref[:, at] = jnp.dot(dz[...], w_held[:, at], preferred_element_type=f32).astype(bf16)
 
     rest[mine] = column[...]
     for p in others("dp"):
@@ -333,15 +336,22 @@
     for p in range(1, rest.shape[0]):
         total = total + rest[p]
     red_ref[...] = total
-    for p in others("dp"):
-        arrival("dp", p, cut_ref.at[p], got_ref.at[p], cut_send, cut_recv).wait_recv()
-    for copy in sent + swaps + spread:
+    for copy in swaps:
+        copy.wait()
+    for copy in sent + spread:
         copy.wait_send()
 
 
-def weight_kernel(scale, toks_ref, got_ref, red_ref, gw_ref, taps_ref, term, land, total, send, recv, tap_send, tap_recv):
+def weight_kernel(scale, parts, *refs):
+    toks = refs[:parts]
+    (got_ref, red_ref, gw_ref, taps_ref, term, pairs, land, total,
+     pair_send, pair_recv, send, recv, tap_send, tap_recv) = refs[parts:]
     me = lax.axis_index("ctx")
     devices, own, _ = term.shape
+    half = devices // 2
+    side = lax.rem(me, 2)
+    seat = me // 2
+    partner = me + 1 - 2 * side
     per = 16 // math.gcd(own, 16)
     count = devices // per
     greet(["ctx"])
@@ -350,29 +360,65 @@
         copy.start()
     taps_ref[me] = red_ref[...]
 
+    def handover(q, target):
+        return pltpu.make_async_remote_copy(
+            src_ref=term.at[target], dst_ref=pairs.at[q], send_sem=pair_send.at[q], recv_sem=pair_recv.at[q],
+            device_id={"ctx": partner}, device_id_type=pl.DeviceIdType.MESH)
+
+    def delivery(q, slot):
+        return pltpu.make_async_remote_copy(
+            src_ref=term.at[2 * q + side], dst_ref=land.at[slot], send_sem=send.at[q], recv_sem=recv.at[slot],
+            device_id={"ctx": 2 * q + side}, device_id_type=pl.DeviceIdType.MESH)
+
     @pl.loop(0, count)
     def _(i):
-        block = lax.rem(me // per + 1 + i, count)
+        if per == 1:
+            second = i // half
+            block = 2 * lax.rem(seat + 1 + lax.rem(i, half), half) + (1 - side) + second * (2 * side - 1)
+        else:
+            block = i
         at = pl.ds(pl.multiple_of(block * (own * per), 16), own * per)
-        piece = jnp.dot(toks_ref[at, :], got_ref[...], preferred_element_type=f32)
+        rows = jnp.concatenate([tok[at, :] for tok in toks], axis=1)
+        piece = jnp.dot(rows, got_ref[...], preferred_element_type=f32)
         for s in range(per):
             target = block * per + s
             term[target] = piece[s * own : (s + 1) * own].astype(bf16)
 
-            @pl.when(target != me)
+            @pl.when(lax.rem(target, 2) != side)
             def _():
-                push("ctx", target, term.at[target], land.at[me], send, recv).start()
-
-    total[...] = term[me].astype(f32)
-    for p in others("ctx"):
-        arrival("ctx", p, term.at[p], land.at[p], send, recv).wait_recv()
-        total[...] += land[p].astype(f32)
+                handover(target // 2, target).start()
+
+    @pl.loop(1, half)
+    def _(j):
+        q = lax.rem(seat + j, half)
+        target = 2 * q + side
+        handover(q, target).wait_recv()
+        term[target] = (term[target].astype(f32) + pairs[q].astype(f32)).astype(bf16)
+        delivery(q, seat).start()
+
+    handover(seat, me).wait_recv()
+    total[...] = term[me].astype(f32) + pairs[seat].astype(f32)
+
+    @pl.loop(1, half)
+    def _(j):
+        q = lax.rem(seat + j, half)
+        delivery(q, q).wait_recv()
+        total[...] += land[q].astype(f32)
+
     gw_ref[...] = (total[...] * scale).astype(bf16)
     for p in others("ctx"):
         arrival("ctx", p, red_ref, taps_ref.at[p], tap_send, tap_recv).wait_recv()
-        arrival("ctx", p, term.at[p], land.at[p], send, recv).wait_send()
     for copy in sent:
         copy.wait_send()
+
+    @pl.loop(1, half)
+    def _(j):
+        q = lax.rem(seat + j, half)
+        delivery(q, q).wait_send()
+
+    @pl.loop(0, half)
+    def _(q):
+        handover(q, 2 * q + 1 - side).wait_send()
 
 
 def shape(dims, kind=f32):
@@ -403,12 +449,6 @@
             vmem_limit_bytes=48 << 20, collective_id=number, has_side_effects=True),
         cost_estimate=pl.CostEstimate(flops=flops, bytes_accessed=1 << 22, transcendentals=0),
     )(*ops)
-
-
-def shifted(block, axis, distance):
-    devices = range(lax.axis_size(axis))
-    route = [(i - distance, i) for i in devices if i - distance in devices]
-    return lax.ppermute(block, axis, route)
 
 
 def local(tokens, w_in, conv_taps, residues, rates, cotangent):
@@ -445,14 +485,18 @@
         [shape((3, rows, wide)), shape((2 * rows, wide)), shape((2 * rows, wide)), shape((2 * modes, wide))],
         [(HALO + rows, chans), (rows, chans)],
         (z, conv_taps, cot, rate_t))
-    inner_f, inner_b, near, every, toks = exchange(
+    turned = feats.T
+    toks = [turned]
+    for j in range(1, dp):
+        route = [(i, (i + j) % dp) for i in range(dp)]
+        toks.append(lax.ppermute(turned, "dp", route))
+    inner_f, inner_b, near, every = exchange(
         inner_kernel, 1,
-        [shape((rows, wide)), shape((rows, wide)), shape((modes, wide)), shape((ctx, 2 * modes, wide)),
-         shape((depth, dp * rows), bf16)],
+        [shape((rows, wide)), shape((rows, wide)), shape((modes, wide)), shape((ctx, 2 * modes, wide))],
         [pltpu.VMEM((rows, wide), f32), pltpu.VMEM((rows, wide), f32),
          pltpu.VMEM((SUB, 2 * rows, LANES), f32), pltpu.VMEM((SUB, 2 * rows, LANES), f32),
-         dma((ctx,)), dma((ctx,)), dma((dp,)), dma((dp,))],
-        (up, gp, rate_t, reff_t, eh, feats.T), flops=5 * 10**9)
+         dma((ctx,)), dma((ctx,))],
+        (up, gp, rate_t, reff_t, eh), flops=5 * 10**9)
     output, dmixed, stat = call(
         functools.partial(join_kernel, width),
         [shape((rows, width), bf16), shape((rows, chans), bf16),
@@ -461,28 +505,25 @@
          (count + 1, chans), (modes, wide)],
         (me.reshape(1), qkv, inner_f, inner_b, near, cot, rate_t, reff_t, every, z), scalars=1)
 
-    after = shifted(dmixed[:HALO], "ctx", -1)
-    dz, cut = call(
-        dz_kernel,
-        [shape((rows, chans), bf16), shape((dp, rows, chans // dp), bf16)],
-        [(rows + HALO, chans), (rows, chans)],
-        (dmixed, after, conv_taps))
-
     piece = chans // dp
     own_feats = depth // ctx
     unit = (SUB + modes, chans // ctx)
     got, grad_feats, red = exchange(
         tokens_kernel, 2,
         [shape((dp, rows, piece), bf16), shape((rows, depth), bf16), shape(unit)],
-        [pltpu.VMEM((depth, chans), bf16), pltpu.VMEM((ctx,) + unit, f32), pltpu.VMEM(unit, f32),
-         pltpu.VMEM((dp,) + unit, f32), dma, dma((dp,)), dma((dp,)), dma((ctx,)), dma((ctx,)), dma((dp,)), dma((dp,))],
-        (dz, cut, stat, w_in), anywhere=(3,))
+        [pltpu.VMEM((chans, depth), bf16), pltpu.VMEM((HALO, chans), bf16), pltpu.VMEM((rows, chans), bf16),
+         pltpu.VMEM((dp, rows, piece), bf16), pltpu.VMEM((rows + HALO, chans), f32), pltpu.VMEM((rows, chans), f32),
+         pltpu.VMEM((ctx,) + unit, f32), pltpu.VMEM(unit, f32), pltpu.VMEM((dp,) + unit, f32),
+         dma, dma, dma, dma((dp,)), dma((dp,)), dma((ctx,)), dma((ctx,)), dma((dp,)), dma((dp,))],
+        (dmixed, conv_taps, stat, w_in.T), anywhere=(3,))
+    half = ctx // 2
     grad_weight, taps = exchange(
-        functools.partial(weight_kernel, scale), 3,
+        functools.partial(weight_kernel, scale, dp), 3,
         [shape((own_feats, piece), bf16), shape((ctx,) + unit)],
-        [pltpu.VMEM((ctx, own_feats, piece), bf16), pltpu.VMEM((ctx, own_feats, piece), bf16),
-         pltpu.VMEM((own_feats, piece), f32), dma((ctx,)), dma((ctx,)), dma((ctx,)), dma((ctx,))],
-        (toks, got.reshape(dp * rows, piece), red))
+        [pltpu.VMEM((ctx, own_feats, piece), bf16), pltpu.VMEM((half, own_feats, piece), bf16),
+         pltpu.VMEM((half, own_feats, piece), bf16), pltpu.VMEM((own_feats, piece), f32),
+         dma((half,)), dma((half,)), dma((half,)), dma((half,)), dma((ctx,)), dma((ctx,))],
+        (*toks, got.reshape(dp * rows, piece), red))
     grad_taps = taps[:, :count].transpose(1, 0, 2).reshape(count, chans) * scale
     grad_residues = amp * red[SUB:, :own].T * scale
     return (output[None], grad_feats[None], grad_weight, grad_taps, grad_residues)

time: 146 us -> 111 us (0.76)
  Pallas kernels: 114 us -> 81 us
  local copies, waits for them, and re-layouts: 19.5 us -> 12.8 us
  starting transfers between devices: 1.47 us -> 7.01 us
    pallas_call x4, Pallas kernels: 104 us -> 72.3 us  [exchange(): pl.pallas_call(kernel, out_shape=outs, in_specs=specs, out_specs=[VM] * l...]
    unnamed x18 -> x31, local copies, waits for them, and re-layouts: 18.3 us -> 11 us
    ppermute x1 -> x3, starting transfers between devices: 1.47 us -> 7.01 us  [local(): toks.append(lax.ppermute(turned, 'dp', route))]
    pallas_call x3 -> x2, Pallas kernels: 10.5 us -> 8.7 us  [call(): pl.pallas_call(kernel, out_shape=outs, in_specs=[SM] * scalars + [VM] * (...]
  transfers between devices with their start and end apart: 1 -> 3, of which waited for: 0 -> 0; matrix products, arithmetic and copies ran while one was open for 9% -> 10% of each run, Pallas kernels for 0% -> 55%
where the time goes in v3:
time: 111 us; the launch traced here: 110 us
  Pallas kernels  81 us (73%)
  local copies, waits for them, and re-layouts  12.8 us (12%)
  starting transfers between devices  7.01 us (6%)
  matrix products  6.43 us (6%)
  other arithmetic  2.07 us (2%)
    pallas_call x4, Pallas kernels, exchange(): pl.pallas_call(kernel, out_shape=outs, in_specs=specs, out_specs=[VM] * l...  72.3 us
    unnamed x31, local copies, waits for them, and re-layouts  11 us
    pallas_call x2, Pallas kernels, call(): pl.pallas_call(kernel, out_shape=outs, in_specs=[SM] * scalars + [VM] * (...  8.7 us
    ppermute x3, starting transfers between devices, local(): toks.append(lax.ppermute(turned, 'dp', route))  7.01 us
    dot_general x1, matrix products, local(): z = jnp.dot(stacked, w_in, preferred_element_type=f32).astype(bf16)  6.43 us
  transfers between devices with their start and end apart: 3, of which 0 were waited for; matrix products, arithmetic and copies ran while one was open for 10% of the time, Pallas kernels for 55%

profile of v3, /device:TPU:0, one launch (start us, length us, event | category | flops | bytes accessed | tf_op | source)
XLA Modules:
  0.0 110.2 jit_solution(12218632745546967486)
XLA Ops:
  0.6 0.0 copy-start.11
  0.6 1.3 %copy.17 = bf16[1,128,1536]{1,2,0:T(8,128)(2,1)S(1)} copy(bf16[1,128,1536]{2,1,0:T(8,128)(2,1)} %param.6) | data formatting | bytes 786432 | tf_op args[0]
  1.9 3.1 %collective-permute-start = (bf16[1536,128]{1,0:T(8,128)(2,1)S(1)}, bf16[1536,128]{1,0:T(8,128)(2,1)S(1)}, u32[]{:S(2)}, u32[]{:S(2)}) collective-permute-start(bf16[1536,128]{1,0:T(8,128)(2,1)S(1)} %bitcast.21), channel_id=1, source_target_pairs={{0,1},{1,2},{2,3},{3,0},{4,5},{5,6},{6,7},{7,4},{8,9},{9,10},{10,1... | collective-permute-start | bytes 1179656 | tf_op jit(solution)/shard_map/ppermute | solution.py:492
  5.0 2.6 %collective-permute-start.1 = (bf16[1536,128]{1,0:T(8,128)(2,1)S(1)}, bf16[1536,128]{1,0:T(8,128)(2,1)}, u32[]{:S(2)}, u32[]{:S(2)}) collective-permute-start(bf16[1536,128]{1,0:T(8,128)(2,1)S(1)} %bitcast.22), channel_id=1, source_target_pairs={{0,2},{1,3},{2,0},{3,1},{4,6},{5,7},{6,4},{7,5},{8,10},{9,11},{10,... | collective-permute-start | bytes 1179656 | tf_op jit(solution)/shard_map/ppermute | solution.py:492
  7.6 1.3 %collective-permute-start.2 = (bf16[1536,128]{1,0:T(8,128)(2,1)S(1)}, bf16[1536,128]{1,0:T(8,128)(2,1)}, u32[]{:S(2)}, u32[]{:S(2)}) collective-permute-start(bf16[1536,128]{1,0:T(8,128)(2,1)S(1)} %bitcast.23), channel_id=1, source_target_pairs={{0,3},{1,0},{2,1},{3,2},{4,7},{5,4},{6,5},{7,6},{8,11},{9,8},{10,9... | collective-permute-start | bytes 1179656 | tf_op jit(solution)/shard_map/ppermute | solution.py:492
  8.9 0.7 multiply_bitcast_fusion.1
  9.7 0.7 pad_maximum_fusion.modal_ref
  10.4 0.0 copy-start
  10.4 1.0 copy-done
  11.4 5.8 %shard_map.101 = (bf16[16,1536]{1,0:T(8,128)(2,1)S(1)}, f32[8,32,120]{2,1,0:T(8,128)S(1)}) custom-call(bf16[128,1536]{1,0:T(8,128)(2,1)S(1)} %bitcast.28, f32[32,120]{1,0:T(8,128)S(1)} %pad_maximum_fusion.modal_ref), custom_call_target="tpu_custom_call" | custom-call | flops 100000000 | bytes 4194304 | tf_op jit(solution)/shard_map/pallas_call | solution.py:442
  17.2 0.1 copy.21
  17.3 0.1 reshape.23
  17.4 0.6 pad_slice_fusion
  18.0 0.2 copy.19
  18.2 0.0 copy-done.11
  18.2 0.1 copy.20
  18.4 0.0 copy-start.4
  18.4 0.0 copy-start.6
  18.4 6.4 %convolution_convert_fusion.z_ref = bf16[144,2880]{1,0:T(8,128)(2,1)S(1)} fusion(bf16[1536,2880]{0,1:T(8,128)(2,1)} %param.7, bf16[128,1536]{0,1:T(8,128)(2,1)S(1)} %bitcast.24, bf16[16,1536]{0,1:T(8,128)(2,1)S(1)} %copy.19), kind=kOutput, calls=%fused_computation | convolution fusion | flops 1275319296 | bytes 10119168 | tf_op jit(solution)/shard_map/dot_general | solution.py:481
  24.9 0.0 copy-done.4
  24.9 3.3 %shard_map.102 = (f32[3,128,1024]{2,1,0:T(8,128)S(1)}, f32[256,1024]{1,0:T(8,128)S(1)}, f32[256,1024]{1,0:T(8,128)S(1)}, f32[32,1024]{1,0:T(8,128)S(1)}) custom-call(bf16[144,2880]{1,0:T(8,128)(2,1)S(1)} %convolution_convert_fusion.z_ref, f32[7,2880]{1,0:T(8,128)S(1)} %copy-done.4, bf16[128,960]{1,0:T(8,128)(2,1)S(1)} %bitcast.26, ...), custom_call_target="tpu_custom_call" | custom-call | flops 100000000 | bytes 4194304 | tf_op jit(solution)/shard_map/pallas_call | solution.py:429
  28.2 0.0 copy-start.1
  28.2 1.2 %copy-done.1 = f32[3,128,1024]{2,1,0:T(8,128)} copy-done((f32[3,128,1024]{2,1,0:T(8,128)}, f32[3,128,1024]{2,1,0:T(8,128)S(1)}, u32[]{:S(2)}) %copy-start.1) | copy-done | bytes 1572888
  29.4 0.0 copy-done.6
  29.4 17.2 %shard_map.103 = (f32[128,1024]{1,0:T(8,128)S(1)}, f32[128,1024]{1,0:T(8,128)S(1)}, f32[16,1024]{1,0:T(8,128)S(1)}, f32[8,32,1024]{2,1,0:T(8,128)S(1)}) custom-call(f32[256,1024]{1,0:T(8,128)S(1)} %get-tuple-element.26.up_ref, f32[256,1024]{1,0:T(8,128)S(1)} %get-tuple-element.27.gp_ref, f32[16,1024]{1,0:T(8,128)S(1)} %get-tuple-element.52.rate_ref, ...), custom_call_target="tpu_custom_call" | custom-call | flops 5000000000 | bytes 4194304 | tf_op jit(solution)/shard_map/pallas_call | solution.py:442
  46.6 0.0 copy-start.2
  46.6 0.8 copy-done.2
  47.4 0.0 copy-start.9
  47.4 0.6 copy-done.9
  48.0 0.0 copy-start.3
  48.0 1.0 copy-done.3
  49.1 0.0 copy-start.7
  49.1 0.8 copy-done.7
  49.9 0.0 copy-start.10
  49.9 0.8 copy-done.10
  50.8 0.0 copy-start.5
  50.8 5.4 %shard_map.104 = (bf16[128,960]{1,0:T(8,128)(2,1)S(1)}, bf16[128,2880]{1,0:T(8,128)(2,1)S(1)}, f32[8,24,360]{2,1,0:T(8,128)S(1)}) custom-call(s32[1]{0:T(128)} %bitcast.me_ref, f32[3,128,1024]{2,1,0:T(8,128)} %copy-done.1, f32[128,1024]{1,0:T(8,128)S(1)} %get-tuple-element.29.inf_ref, f32[128,1024]{1,0:T(8,128)S(1)} %copy-done.3, f32[16,1024]{1,0:T(8,128)S(1)} %copy-done.10, ...), custom_call_target="tpu_custom_call" | custom-call | flops 100000000 | bytes 4194304 | tf_op jit(solution)/shard_map/pallas_call | solution.py:429
  56.1 0.0 copy-start.8
  56.1 0.0 copy-done.5
  56.2 0.0 copy-start.12
  56.2 28.4 %shard_map.105 = (bf16[4,128,720]{2,1,0:T(8,128)(2,1)S(1)}, bf16[128,1536]{1,0:T(8,128)(2,1)S(1)}, f32[24,360]{1,0:T(8,128)S(1)}) custom-call(bf16[128,2880]{1,0:T(8,128)(2,1)S(1)} %get-tuple-element.34.dm_ref, f32[7,2880]{1,0:T(8,128)S(1)} %copy-done.5, f32[8,24,360]{2,1,0:T(8,128)S(1)} %get-tuple-element.35.stat_ref, bf16[2880,1536]{1,0:T(8,128)(2,1)} %bitcast.33), custom_call_target="tpu_custom_call" | custom-call | flops 100000000 | bytes 4194304 | tf_op jit(solution)/shard_map/pallas_call | solution.py:442
  84.5 0.0 copy-done.8
  84.5 1.8 %copy.23 = bf16[1,128,960]{1,2,0:T(8,128)(2,1)} copy(bf16[1,128,960]{2,1,0:T(8,128)(2,1)} %bitcast.31) | data formatting | bytes 491520
  86.3 0.0 copy-done.12
  86.3 0.6 fusion.3
  87.0 0.0 collective-permute-done.refs_1_
  87.0 0.0 collective-permute-done.1.refs_2_
  87.0 0.0 collective-permute-done.2.refs_3_
  87.0 20.9 %shard_map.106 = (bf16[192,720]{1,0:T(8,128)(2,1)S(1)}, f32[8,24,360]{2,1,0:T(8,128)S(1)}) custom-call(bf16[1536,128]{1,0:T(8,128)(2,1)S(1)} %bitcast.25, bf16[1536,128]{1,0:T(8,128)(2,1)S(1)} %collective-permute-done.refs_1_, bf16[1536,128]{1,0:T(8,128)(2,1)} %collective-permute-done.1.refs_2_, bf16[1536,128]{1,0:T(8,128)(2,1)} %collective-permute-done.2.refs_3_, ...), custom_call_target="tpu_custom_call" | custom-call | flops 100000000 | bytes 4194304 | tf_op jit(solution)/shard_map/pallas_call | solution.py:442
  108.0 0.7 mul.36
  108.7 0.7 copy.27
  109.5 0.7 copy.28
  (2 shorter events, 0.0 us)
Async XLA Ops:
  0.6 17.6 %copy-start.11 = (bf16[1,128,960]{1,2,0:T(8,128)(2,1)S(1)}, bf16[1,128,960]{1,2,0:T(8,128)(2,1)}, u32[]{:S(2)}) copy-start(bf16[1,128,960]{1,2,0:T(8,128)(2,1)} %param.11) | copy-start | bytes 737284
  1.9 85.1 %collective-permute-start = (bf16[1536,128]{1,0:T(8,128)(2,1)S(1)}, bf16[1536,128]{1,0:T(8,128)(2,1)S(1)}, u32[]{:S(2)}, u32[]{:S(2)}) collective-permute-start(bf16[1536,128]{1,0:T(8,128)(2,1)S(1)} %bitcast.21), channel_id=1, source_target_pairs={{0,1},{1,2},{2,3},{3,0},{4,5},{5,6},{6,7},{7,4},{8,9},{9,10},{10,1... | collective-permute-start | bytes 1179656 | tf_op jit(solution)/shard_map/ppermute | solution.py:492
  5.0 82.0 %collective-permute-start.1 = (bf16[1536,128]{1,0:T(8,128)(2,1)S(1)}, bf16[1536,128]{1,0:T(8,128)(2,1)}, u32[]{:S(2)}, u32[]{:S(2)}) collective-permute-start(bf16[1536,128]{1,0:T(8,128)(2,1)S(1)} %bitcast.22), channel_id=1, source_target_pairs={{0,2},{1,3},{2,0},{3,1},{4,6},{5,7},{6,4},{7,5},{8,10},{9,11},{10,... | collective-permute-start | bytes 1179656 | tf_op jit(solution)/shard_map/ppermute | solution.py:492
  7.6 79.4 %collective-permute-start.2 = (bf16[1536,128]{1,0:T(8,128)(2,1)S(1)}, bf16[1536,128]{1,0:T(8,128)(2,1)}, u32[]{:S(2)}, u32[]{:S(2)}) collective-permute-start(bf16[1536,128]{1,0:T(8,128)(2,1)S(1)} %bitcast.23), channel_id=1, source_target_pairs={{0,3},{1,0},{2,1},{3,2},{4,7},{5,4},{6,5},{7,6},{8,11},{9,8},{10,9... | collective-permute-start | bytes 1179656 | tf_op jit(solution)/shard_map/ppermute | solution.py:492
  10.4 1.0 copy-start
  18.4 6.5 %copy-start.4 = (f32[7,2880]{1,0:T(8,128)S(1)}, f32[7,2880]{1,0:T(8,128)}, u32[]{:S(2)}) copy-start(f32[7,2880]{1,0:T(8,128)} %taps_ref.3) | copy-start | bytes 241924
  18.4 11.0 %copy-start.6 = (f32[16,1024]{1,0:T(8,128)S(1)}, f32[16,1024]{1,0:T(8,128)}, u32[]{:S(2)}) copy-start(f32[16,1024]{1,0:T(8,128)} %get-tuple-element.51.reff_ref) | copy-start | bytes 196612
  28.2 1.2 %copy-start.1 = (f32[3,128,1024]{2,1,0:T(8,128)}, f32[3,128,1024]{2,1,0:T(8,128)S(1)}, u32[]{:S(2)}) copy-start(f32[3,128,1024]{2,1,0:T(8,128)S(1)} %get-tuple-element.25.qkv_ref) | copy-start | bytes 4718596
  46.6 0.8 copy-start.2
  47.4 0.6 copy-start.9
  48.0 1.0 copy-start.3
  49.1 0.8 copy-start.7
  49.9 0.8 copy-start.10
  50.8 5.4 %copy-start.5 = (f32[7,2880]{1,0:T(8,128)S(1)}, f32[7,2880]{1,0:T(8,128)}, u32[]{:S(2)}) copy-start(f32[7,2880]{1,0:T(8,128)} %taps_ref.3) | copy-start | bytes 241924
  56.1 28.4 %copy-start.8 = (bf16[128,960]{1,0:T(8,128)(2,1)}, bf16[128,960]{1,0:T(8,128)(2,1)S(1)}, u32[]{:S(2)}) copy-start(bf16[128,960]{1,0:T(8,128)(2,1)S(1)} %get-tuple-element.33) | copy-start | bytes 737284
  56.2 30.2 %copy-start.12 = (f32[120,16]{0,1:T(8,128)S(1)}, f32[120,16]{0,1:T(8,128)}, u32[]{:S(2)}) copy-start(f32[120,16]{0,1:T(8,128)} %param.10) | copy-start | bytes 23044

commit v4 on v3

--- a/solution.py
+++ b/solution.py
@@ -14,8 +14,6 @@
 GROUP = 32
 
 VM = pl.BlockSpec(memory_space=pltpu.VMEM)
-SM = pl.BlockSpec(memory_space=pltpu.SMEM)
-PARAMS = pltpu.CompilerParams(vmem_limit_bytes=48 << 20)
 f32 = jnp.float32
 bf16 = jnp.bfloat16
 
@@ -142,14 +140,13 @@
                 blocks, 0.0, 1.0, backwards)
 
 
-def join_kernel(width, me_ref, qkv_ref, inf_ref, inb_ref, near_ref, cot_ref, rate_ref, reff_ref, all_ref, z_ref,
-                out_ref, dm_ref, stat_ref, first, last, lf, lb, dm, zs, tap_ref, draw_ref):
+def join_kernel(width, me, qkv_ref, lf, lb, near_ref, cot_ref, rate_ref, reff_ref, all_ref, zs,
+                out_ref, dm_ref, stat_ref, first, last, dm, tap_ref, draw_ref):
     rows = cot_ref.shape[0]
     modes, wide = rate_ref.shape
     blocks = rows // SUB
     devices = all_ref.shape[0]
     count = tap_ref.shape[0] - 1
-    me = me_ref[0]
     rate = rate_ref[...]
     first[...] = jnp.zeros((modes, wide), f32)
     last[...] = jnp.zeros((modes, wide), f32)
@@ -166,8 +163,6 @@
     draw_ref[...] = near_ref[...] + first[...] * all_ref[me, modes : 2 * modes] * jnp.exp(-rate)
     first[...] = first[...] * reff_ref[...]
     last[...] = last[...] * reff_ref[...]
-    lf[...] = inf_ref[...]
-    lb[...] = inb_ref[...]
 
     @pl.loop(0, wide // LANES)
     def _(tile):
@@ -187,7 +182,6 @@
         held = dm[:, a:b].astype(bf16)
         dm_ref[:, a:b] = held
         held = held.astype(f32)
-        zs[:, a:b] = z_ref[:, a:b].astype(f32)
         for j in range(count):
             tap_ref[j : j + 1, a:b] = jnp.sum(
                 held * zs[HALO - j : HALO - j + rows, a:b], axis=0, keepdims=True)
@@ -243,55 +237,12 @@
         device_id={axis: peer}, device_id_type=pl.DeviceIdType.MESH)
 
 
-def start_kernel(feats_ref, modal_ref, halo_ref, all_ref, send, recv, hop_send, hop_recv):
-    me = lax.axis_index("ctx")
-    size = lax.axis_size("ctx")
-    rows = feats_ref.shape[0]
-    greet(["ctx"])
-    hop = pltpu.make_async_remote_copy(
-        src_ref=feats_ref.at[pl.ds(rows - HALO, HALO)], dst_ref=halo_ref, send_sem=hop_send, recv_sem=hop_recv,
-        device_id={"ctx": lax.rem(me + 1, size)}, device_id_type=pl.DeviceIdType.MESH)
-    hop.start()
-    sent = [push("ctx", p, modal_ref, all_ref.at[me], send, recv) for p in others("ctx")]
-    for copy in sent:
-        copy.start()
-    all_ref[me] = modal_ref[...]
-    hop.wait()
-
-    @pl.when(me == 0)
-    def _():
-        halo_ref[...] = jnp.zeros(halo_ref.shape, halo_ref.dtype)
-
-    for p in others("ctx"):
-        arrival("ctx", p, modal_ref, all_ref.at[p], send, recv).wait_recv()
-    for copy in sent:
-        copy.wait_send()
-
-
-def inner_kernel(up_ref, gp_ref, rate_ref, reff_ref, eh_ref, inf_ref, inb_ref, near_ref, all_ref,
-                 filt, corr, ups, gps, send, recv):
-    me = lax.axis_index("ctx")
-    greet(["ctx"])
-    sent = [push("ctx", p, eh_ref, all_ref.at[me], send, recv) for p in others("ctx")]
-    for copy in sent:
-        copy.start()
-    all_ref[me] = eh_ref[...]
-    near_kernel(up_ref, gp_ref, rate_ref, reff_ref, inf_ref, inb_ref, near_ref, filt, corr, ups, gps)
-    for p in others("ctx"):
-        arrival("ctx", p, eh_ref, all_ref.at[p], send, recv).wait_recv()
-    for copy in sent:
-        copy.wait_send()
-
-
-def tokens_kernel(dm_ref, taps_ref, stat_ref, w_ref, got_ref, feats_ref, red_ref,
-                  w_held, after, dz, cut, pad, full, parts, column, rest, w_sem, hop_send, hop_recv,
+def tokens_part(dm_ref, taps_ref, stat_ref, w_held, got_ref, feats_ref, red_ref,
+                  after, dz, cut, pad, full, parts, column, rest, hop_send, hop_recv,
                   cut_send, cut_recv, st_send, st_recv, col_send, col_recv):
     me = lax.axis_index("ctx")
     size = lax.axis_size("ctx")
     mine = lax.axis_index("dp")
-    load = pltpu.make_async_copy(w_ref, w_held, w_sem)
-    load.start()
-    greet(["ctx", "dp"])
     hop = pltpu.make_async_remote_copy(
         src_ref=dm_ref.at[pl.ds(0, HALO)], dst_ref=after, send_sem=hop_send, recv_sem=hop_recv,
         device_id={"ctx": lax.rem(me + size - 1, size)}, device_id_type=pl.DeviceIdType.MESH)
@@ -321,7 +272,6 @@
     spread = [push("dp", p, column, rest.at[mine], col_send, col_recv) for p in others("dp")]
     for copy in spread:
         copy.start()
-    load.wait()
     tile = 2 * LANES
 
     @pl.loop(0, w_held.shape[1] // tile)
@@ -342,10 +292,8 @@
         copy.wait_send()
 
 
-def weight_kernel(scale, parts, *refs):
-    toks = refs[:parts]
-    (got_ref, red_ref, gw_ref, taps_ref, term, pairs, land, total,
-     pair_send, pair_recv, send, recv, tap_send, tap_recv) = refs[parts:]
+def weight_part(scale, toks, got_ref, red_ref, gw_ref, taps_ref, term, pairs, land, total,
+                pair_send, pair_recv, send, recv, tap_send, tap_recv):
     me = lax.axis_index("ctx")
     devices, own, _ = term.shape
     half = devices // 2
@@ -354,7 +302,7 @@
     partner = me + 1 - 2 * side
     per = 16 // math.gcd(own, 16)
     count = devices // per
-    greet(["ctx"])
+    depth = got_ref.shape[0] * got_ref.shape[1]
     sent = [push("ctx", p, red_ref, taps_ref.at[me], tap_send, tap_recv) for p in others("ctx")]
     for copy in sent:
         copy.start()
@@ -378,8 +326,8 @@
         else:
             block = i
         at = pl.ds(pl.multiple_of(block * (own * per), 16), own * per)
-        rows = jnp.concatenate([tok[at, :] for tok in toks], axis=1)
-        piece = jnp.dot(rows, got_ref[...], preferred_element_type=f32)
+        rows = jnp.concatenate([toks[j, at, :] for j in range(toks.shape[0])], axis=1)
+        piece = jnp.dot(rows, got_ref[...].reshape(depth, -1), preferred_element_type=f32)
         for s in range(per):
             target = block * per + s
             term[target] = piece[s * own : (s + 1) * own].astype(bf16)
@@ -425,30 +373,84 @@
     return jax.ShapeDtypeStruct(dims, kind)
 
 
-def call(kernel, outs, scratch, ops, scalars=0, flops=10**8):
-    return pl.pallas_call(
-        kernel,
-        out_shape=outs,
-        in_specs=[SM] * scalars + [VM] * (len(ops) - scalars),
-        out_specs=[VM] * len(outs),
-        scratch_shapes=[pltpu.VMEM(dims, f32) for dims in scratch],
-        compiler_params=PARAMS,
-        cost_estimate=pl.CostEstimate(flops=flops, bytes_accessed=1 << 22, transcendentals=0),
-    )(*ops)
-
-
-def exchange(kernel, number, outs, scratch, ops, anywhere=(), flops=10**8):
-    specs = [pl.BlockSpec(memory_space=pl.ANY) if i in anywhere else VM for i in range(len(ops))]
-    return pl.pallas_call(
-        kernel,
-        out_shape=outs,
-        in_specs=specs,
-        out_specs=[VM] * len(outs),
-        scratch_shapes=scratch,
-        compiler_params=pltpu.CompilerParams(
-            vmem_limit_bytes=48 << 20, collective_id=number, has_side_effects=True),
-        cost_estimate=pl.CostEstimate(flops=flops, bytes_accessed=1 << 22, transcendentals=0),
-    )(*ops)
+def operator_kernel(width, scale, feats_ref, taps_ref, cot_ref, modal_ref, w_ref,
+                    out_ref, gf_ref, gw_ref, gt_ref, red_ref,
+                    w_held, stack, toks, modal_all, rate, reff, z, zs, mixed, qkv, up, gp, eh, every,
+                    inf, inb, near, filt, corr, ups, gps, first, last, dm, dm16, tap, draw, stat,
+                    after, dz, cut, full, parts, column, rest, got, term, pairs, land, total, taps_all,
+                    w_sem, hop_send, hop_recv, tok_send, tok_recv, mod_send, mod_recv, st_send, st_recv,
+                    aft_send, aft_recv, cut_send, cut_recv, part_send, part_recv, col_send, col_recv,
+                    pair_send, pair_recv, land_send, land_recv, tap_send, tap_recv):
+    me = lax.axis_index("ctx")
+    size = lax.axis_size("ctx")
+    rows, depth = feats_ref.shape
+    chans = w_held.shape[0]
+    modes, wide = rate.shape
+    own = width // size
+    count = taps_ref.shape[0]
+    cuts = [(a, min(a + 6 * LANES, chans)) for a in range(0, chans, 6 * LANES)]
+    loads = [pltpu.make_async_copy(w_ref.at[a:b], w_held.at[a:b], w_sem.at[i]) for i, (a, b) in enumerate(cuts)]
+    for copy in loads:
+        copy.start()
+    greet(["ctx", "dp"])
+    hop = pltpu.make_async_remote_copy(
+        src_ref=feats_ref.at[pl.ds(rows - HALO, HALO)], dst_ref=stack.at[pl.ds(0, HALO)],
+        send_sem=hop_send, recv_sem=hop_recv,
+        device_id={"ctx": lax.rem(me + 1, size)}, device_id_type=pl.DeviceIdType.MESH)
+    hop.start()
+    sent = [push("ctx", p, modal_ref, modal_all.at[me], mod_send, mod_recv) for p in others("ctx")]
+    for copy in sent:
+        copy.start()
+    for a, b in lane_tiles(depth):
+        toks[0, a:b, :] = feats_ref[:, a:b].astype(f32).T.astype(bf16)
+    swaps = []
+    for j, p in enumerate(others("dp")):
+        swaps.append(pltpu.make_async_remote_copy(
+            src_ref=toks.at[0], dst_ref=toks.at[j + 1], send_sem=tok_send.at[j], recv_sem=tok_recv.at[j],
+            device_id={"dp": p}, device_id_type=pl.DeviceIdType.MESH))
+        swaps[-1].start()
+    stack[HALO:, :] = feats_ref[...]
+    hop.wait()
+
+    @pl.when(me == 0)
+    def _():
+        stack[0:HALO, :] = jnp.zeros((HALO, depth), bf16)
+
+    for i, (a, b) in enumerate(cuts):
+        loads[i].wait()
+        z[:, a:b] = lax.dot_general(
+            stack[...], w_held[a:b, :], (((1,), (1,)), ((), ())), preferred_element_type=f32).astype(bf16)
+    modal_all[me] = modal_ref[...]
+    for p in others("ctx"):
+        arrival("ctx", p, modal_ref, modal_all.at[p], mod_send, mod_recv).wait_recv()
+    rate[...] = jnp.zeros((modes, wide), f32)
+    reff[...] = jnp.zeros((modes, wide), f32)
+    for d in range(size):
+        rate[:, d * own : (d + 1) * own] = modal_all[d, 0:modes]
+        reff[:, d * own : (d + 1) * own] = modal_all[d, modes : 2 * modes]
+
+    states_kernel(width, z, taps_ref, cot_ref, rate, qkv, up, gp, eh, zs, mixed)
+    flow = [push("ctx", p, eh, every.at[me], st_send, st_recv) for p in others("ctx")]
+    for copy in flow:
+        copy.start()
+    every[me] = eh[...]
+    near_kernel(up, gp, rate, reff, inf, inb, near, filt, corr, ups, gps)
+    for p in others("ctx"):
+        arrival("ctx", p, eh, every.at[p], st_send, st_recv).wait_recv()
+    join_kernel(width, me, qkv, inf, inb, near, cot_ref, rate, reff, every, zs,
+                out_ref, dm16, stat, first, last, dm, tap, draw)
+    tokens_part(dm16, taps_ref, stat, w_held, got, gf_ref, red_ref,
+                after, dz, cut, zs, full, parts, column, rest, aft_send, aft_recv,
+                cut_send, cut_recv, part_send, part_recv, col_send, col_recv)
+    for copy in swaps:
+        copy.wait()
+    weight_part(scale, toks, got, red_ref, gw_ref, taps_all, term, pairs, land, total,
+                pair_send, pair_recv, land_send, land_recv, tap_send, tap_recv)
+    unit = chans // size
+    for d in range(size):
+        gt_ref[:, d * unit : (d + 1) * unit] = taps_all[d, 0:count, :] * scale
+    for copy in sent + flow:
+        copy.wait_send()
 
 
 def local(tokens, w_in, conv_taps, residues, rates, cotangent):
@@ -466,65 +468,46 @@
     wide = -(-width // LANES) * LANES
 
     amp = jnp.sqrt(-jnp.expm1(-2.0 * rates))
+    modal = jnp.concatenate([rates.T, (residues * amp).T], axis=0)
     dma = pltpu.SemaphoreType.DMA
-    modal = jnp.concatenate([rates.T, (residues * amp).T], axis=0)
-    before, modal = exchange(
-        start_kernel, 0,
-        [shape((HALO, depth), bf16), shape((ctx, 2 * modes, own))],
-        [dma((ctx,)), dma((ctx,)), dma, dma],
-        (feats, modal))
-    modal = modal.transpose(1, 0, 2).reshape(2 * modes, width)
-    modal = jnp.pad(modal, ((0, 0), (0, wide - width)))
-    rate_t, reff_t = modal[:modes], modal[modes:]
-
-    stacked = jnp.concatenate([before, feats], axis=0)
-    z = jnp.dot(stacked, w_in, preferred_element_type=f32).astype(bf16)
-
-    qkv, up, gp, eh = call(
-        functools.partial(states_kernel, width),
-        [shape((3, rows, wide)), shape((2 * rows, wide)), shape((2 * rows, wide)), shape((2 * modes, wide))],
-        [(HALO + rows, chans), (rows, chans)],
-        (z, conv_taps, cot, rate_t))
-    turned = feats.T
-    toks = [turned]
-    for j in range(1, dp):
-        route = [(i, (i + j) % dp) for i in range(dp)]
-        toks.append(lax.ppermute(turned, "dp", route))
-    inner_f, inner_b, near, every = exchange(
-        inner_kernel, 1,
-        [shape((rows, wide)), shape((rows, wide)), shape((modes, wide)), shape((ctx, 2 * modes, wide))],
-        [pltpu.VMEM((rows, wide), f32), pltpu.VMEM((rows, wide), f32),
-         pltpu.VMEM((SUB, 2 * rows, LANES), f32), pltpu.VMEM((SUB, 2 * rows, LANES), f32),
-         dma((ctx,)), dma((ctx,))],
-        (up, gp, rate_t, reff_t, eh), flops=5 * 10**9)
-    output, dmixed, stat = call(
-        functools.partial(join_kernel, width),
-        [shape((rows, width), bf16), shape((rows, chans), bf16),
-         shape((ctx, SUB + modes, chans // ctx))],
-        [(modes, wide), (modes, wide), (rows, wide), (rows, wide), (rows, chans), (HALO + rows, chans),
-         (count + 1, chans), (modes, wide)],
-        (me.reshape(1), qkv, inner_f, inner_b, near, cot, rate_t, reff_t, every, z), scalars=1)
-
     piece = chans // dp
     own_feats = depth // ctx
+    half = ctx // 2
     unit = (SUB + modes, chans // ctx)
-    got, grad_feats, red = exchange(
-        tokens_kernel, 2,
-        [shape((dp, rows, piece), bf16), shape((rows, depth), bf16), shape(unit)],
-        [pltpu.VMEM((chans, depth), bf16), pltpu.VMEM((HALO, chans), bf16), pltpu.VMEM((rows, chans), bf16),
-         pltpu.VMEM((dp, rows, piece), bf16), pltpu.VMEM((rows + HALO, chans), f32), pltpu.VMEM((rows, chans), f32),
-         pltpu.VMEM((ctx,) + unit, f32), pltpu.VMEM(unit, f32), pltpu.VMEM((dp,) + unit, f32),
-         dma, dma, dma, dma((dp,)), dma((dp,)), dma((ctx,)), dma((ctx,)), dma((dp,)), dma((dp,))],
-        (dmixed, conv_taps, stat, w_in.T), anywhere=(3,))
-    half = ctx // 2
-    grad_weight, taps = exchange(
-        functools.partial(weight_kernel, scale, dp), 3,
-        [shape((own_feats, piece), bf16), shape((ctx,) + unit)],
-        [pltpu.VMEM((ctx, own_feats, piece), bf16), pltpu.VMEM((half, own_feats, piece), bf16),
-         pltpu.VMEM((half, own_feats, piece), bf16), pltpu.VMEM((own_feats, piece), f32),
-         dma((half,)), dma((half,)), dma((half,)), dma((half,)), dma((ctx,)), dma((ctx,))],
-        (*toks, got.reshape(dp * rows, piece), red))
-    grad_taps = taps[:, :count].transpose(1, 0, 2).reshape(count, chans) * scale
+
+    def held(*dims):
+        return pltpu.VMEM(dims, f32)
+
+    def short(*dims):
+        return pltpu.VMEM(dims, bf16)
+
+    scratch = [
+        short(chans, depth), short(HALO + rows, depth), short(dp, depth, rows),
+        held(ctx, 2 * modes, own), held(modes, wide), held(modes, wide), short(HALO + rows, chans),
+        held(HALO + rows, chans), held(rows, chans), held(3, rows, wide), held(2 * rows, wide),
+        held(2 * rows, wide), held(2 * modes, wide), held(ctx, 2 * modes, wide),
+        held(rows, wide), held(rows, wide), held(modes, wide), held(rows, wide), held(rows, wide),
+        held(SUB, 2 * rows, LANES), held(SUB, 2 * rows, LANES), held(modes, wide), held(modes, wide),
+        held(rows, chans), short(rows, chans), held(count + 1, chans), held(modes, wide), held(ctx, *unit),
+        short(HALO, chans), short(rows, chans), short(dp, rows, piece), held(rows, chans),
+        held(ctx, *unit), held(*unit), held(dp, *unit), short(dp, rows, piece),
+        short(ctx, own_feats, piece), short(half, own_feats, piece), short(half, own_feats, piece),
+        held(own_feats, piece), held(ctx, *unit),
+        dma((-(-chans // (6 * LANES)),)), dma, dma, dma((dp,)), dma((dp,)), dma((ctx,)), dma((ctx,)),
+        dma((ctx,)), dma((ctx,)), dma, dma, dma((dp,)), dma((dp,)), dma((ctx,)), dma((ctx,)),
+        dma((dp,)), dma((dp,)), dma((half,)), dma((half,)), dma((half,)), dma((half,)), dma((ctx,)), dma((ctx,)),
+    ]
+    output, grad_feats, grad_weight, grad_taps, red = pl.pallas_call(
+        functools.partial(operator_kernel, width, scale),
+        out_shape=[shape((rows, width), bf16), shape((rows, depth), bf16), shape((own_feats, piece), bf16),
+                   shape((count, chans)), shape(unit)],
+        in_specs=[VM] * 4 + [pl.BlockSpec(memory_space=pl.ANY)],
+        out_specs=[VM] * 5,
+        scratch_shapes=scratch,
+        compiler_params=pltpu.CompilerParams(
+            vmem_limit_bytes=56 << 20, collective_id=0, has_side_effects=True),
+        cost_estimate=pl.CostEstimate(flops=10**10, bytes_accessed=1 << 24, transcendentals=0),
+    )(feats, conv_taps, cot, modal, w_in.T)
     grad_residues = amp * red[SUB:, :own].T * scale
     return (output[None], grad_feats[None], grad_weight, grad_taps, grad_residues)
 

time: 111 us -> 94.6 us (0.85)
  starting transfers between devices: 7.01 us -> 0 us
  matrix products: 6.43 us -> 0 us
  local copies, waits for them, and re-layouts: 12.8 us -> 8.58 us
  other arithmetic: 2.07 us -> 3.36 us
    ppermute x3 -> x0, starting transfers between devices: 7.01 us -> none  [local(): toks.append(lax.ppermute(turned, 'dp', route))]
    dot_general x1 -> x0, matrix products: 6.43 us -> none  [local(): z = jnp.dot(stacked, w_in, preferred_element_type=f32).astype(bf16)]
    unnamed x31 -> x7, local copies, waits for them, and re-layouts: 11 us -> 8.58 us
    pallas_call x6 -> x1, Pallas kernels: 81 us -> 81.6 us  [local(): pl.pallas_call(functools.partial(operator_kernel, width, scale), out_shap...]
  transfers between devices with their start and end apart: 3 -> 0, of which waited for: 0 -> 0; matrix products, arithmetic and copies ran while one was open for 10% -> 0% of each run, Pallas kernels for 55% -> 0%
where the time goes in v4:
time: 94.6 us; the launch traced here: 94.1 us
  Pallas kernels  81.6 us (86%)
  local copies, waits for them, and re-layouts  8.58 us (9%)
  other arithmetic  3.36 us (4%)
    pallas_call x1, Pallas kernels, local(): pl.pallas_call(functools.partial(operator_kernel, width, scale), out_shap...  81.6 us
    unnamed x7, local copies, waits for them, and re-layouts  8.58 us

profile of v4, /device:TPU:0, one launch (start us, length us, event | category | flops | bytes accessed | tf_op | source)
XLA Modules:
  0.0 94.1 jit_solution(11151645591046664682)
XLA Ops:
  0.6 0.7 multiply_bitcast_fusion
  1.4 1.3 %pad_maximum_fusion.modal_ref = f32[32,120]{1,0:T(8,128)} fusion(f32[16,120]{1,0:T(8,128)S(1)} %multiply_bitcast_fusion, f32[16,120]{1,0:T(8,128)} %bitcast.15), kind=kLoop, calls=%fused_computation | loop fusion | flops 3840 | bytes 30720 | tf_op jit(solution)/shard_map/concatenate | solution.py:471
  2.7 1.8 %copy.11 = bf16[1,128,960]{2,1,0:T(8,128)(2,1)} copy(bf16[1,128,960]{1,2,0:T(8,128)(2,1)} %param.11) | data formatting | bytes 491520 | tf_op args[5]
  4.5 0.0 copy-start
  4.5 81.6 %shard_map.101 = (bf16[128,960]{1,0:T(8,128)(2,1)}, bf16[128,1536]{1,0:T(8,128)(2,1)}, bf16[192,720]{1,0:T(8,128)(2,1)}, f32[7,2880]{1,0:T(8,128)}, f32[24,360]{1,0:T(8,128)}) custom-call(bf16[128,1536]{1,0:T(8,128)(2,1)} %bitcast.17, f32[7,2880]{1,0:T(8,128)} %taps_ref.1, bf16[128,960]{1,0:T(8,128)(2,1)} %bitcast.14, f32[32,120]{1,0:T(8,128)} %pad_maximum_fusion.modal_ref, ...), custom_call_target="tpu_custom_call" | custom-call | flops 10000000000 | bytes 16777216 | tf_op jit(solution)/shard_map/pallas_call | solution.py:500
  86.0 1.8 %copy.12 = bf16[1,128,960]{1,2,0:T(8,128)(2,1)} copy(bf16[1,128,960]{2,1,0:T(8,128)(2,1)} %bitcast.13) | data formatting | bytes 491520
  87.8 0.0 copy-done
  87.8 1.3 %fusion = f32[120,16]{0,1:T(8,128)} fusion(f32[24,360]{1,0:T(8,128)} %get-tuple-element.14, f32[120,16]{0,1:T(8,128)S(1)} %copy-done), kind=kLoop, calls=%fused_computation.2 | loop fusion | flops 7680 | bytes 23040 | tf_op jit(solution)/shard_map/mul | solution.py:511
  89.2 1.8 %copy.16 = bf16[1,128,1536]{2,1,0:T(8,128)(2,1)} copy(bf16[1,128,1536]{2,1,0:T(8,128)(2,1)} %bitcast.12) | data formatting | bytes 786432
  90.9 1.7 %copy.17 = bf16[192,720]{1,0:T(8,128)(2,1)} copy(bf16[192,720]{1,0:T(8,128)(2,1)} %get-tuple-element.27) | data formatting | bytes 552960
  92.6 1.5 %copy.18 = f32[7,2880]{1,0:T(8,128)} copy(f32[7,2880]{1,0:T(8,128)} %get-tuple-element.28) | data formatting | bytes 161280
Async XLA Ops:
  4.5 83.4 %copy-start = (f32[120,16]{0,1:T(8,128)S(1)}, f32[120,16]{0,1:T(8,128)}, u32[]{:S(2)}) copy-start(f32[120,16]{0,1:T(8,128)} %param.10) | copy-start | bytes 23044

commit v5 on v4

--- a/solution.py
+++ b/solution.py
@@ -11,7 +11,7 @@
 LANES = 128
 SUB = 8
 HALO = 16
-GROUP = 32
+GROUP = 16
 
 VM = pl.BlockSpec(memory_space=pltpu.VMEM)
 f32 = jnp.float32

time: 94.6 us -> 94 us (level)
  no operation moved by 1% of the time
where the time goes in v5:
time: 94 us; the launch traced here: 93.6 us
  Pallas kernels  81 us (86%)
  local copies, waits for them, and re-layouts  8.58 us (9%)
  other arithmetic  3.36 us (4%)
    pallas_call x1, Pallas kernels, local(): pl.pallas_call(functools.partial(operator_kernel, width, scale), out_shap...  81 us
    unnamed x7, local copies, waits for them, and re-layouts  8.58 us

profile of v5, /device:TPU:0, one launch (start us, length us, event | category | flops | bytes accessed | tf_op | source)
XLA Modules:
  0.0 93.6 jit_solution(8174583356034259282)
XLA Ops:
  0.6 0.7 multiply_bitcast_fusion
  1.4 1.3 %pad_maximum_fusion.modal_ref = f32[32,120]{1,0:T(8,128)} fusion(f32[16,120]{1,0:T(8,128)S(1)} %multiply_bitcast_fusion, f32[16,120]{1,0:T(8,128)} %bitcast.15), kind=kLoop, calls=%fused_computation | loop fusion | flops 3840 | bytes 30720 | tf_op jit(solution)/shard_map/concatenate | solution.py:471
  2.7 1.8 %copy.11 = bf16[1,128,960]{2,1,0:T(8,128)(2,1)} copy(bf16[1,128,960]{1,2,0:T(8,128)(2,1)} %param.11) | data formatting | bytes 491520 | tf_op args[5]
  4.5 0.0 copy-start
  4.5 81.0 %shard_map.101 = (bf16[128,960]{1,0:T(8,128)(2,1)}, bf16[128,1536]{1,0:T(8,128)(2,1)}, bf16[192,720]{1,0:T(8,128)(2,1)}, f32[7,2880]{1,0:T(8,128)}, f32[24,360]{1,0:T(8,128)}) custom-call(bf16[128,1536]{1,0:T(8,128)(2,1)} %bitcast.17, f32[7,2880]{1,0:T(8,128)} %taps_ref.1, bf16[128,960]{1,0:T(8,128)(2,1)} %bitcast.14, f32[32,120]{1,0:T(8,128)} %pad_maximum_fusion.modal_ref, ...), custom_call_target="tpu_custom_call" | custom-call | flops 10000000000 | bytes 16777216 | tf_op jit(solution)/shard_map/pallas_call | solution.py:500
  85.5 1.8 %copy.12 = bf16[1,128,960]{1,2,0:T(8,128)(2,1)} copy(bf16[1,128,960]{2,1,0:T(8,128)(2,1)} %bitcast.13) | data formatting | bytes 491520
  87.3 0.0 copy-done
  87.3 1.3 %fusion = f32[120,16]{0,1:T(8,128)} fusion(f32[24,360]{1,0:T(8,128)} %get-tuple-element.14, f32[120,16]{0,1:T(8,128)S(1)} %copy-done), kind=kLoop, calls=%fused_computation.2 | loop fusion | flops 7680 | bytes 23040 | tf_op jit(solution)/shard_map/mul | solution.py:511
  88.6 1.8 %copy.16 = bf16[1,128,1536]{2,1,0:T(8,128)(2,1)} copy(bf16[1,128,1536]{2,1,0:T(8,128)(2,1)} %bitcast.12) | data formatting | bytes 786432
  90.4 1.7 %copy.17 = bf16[192,720]{1,0:T(8,128)(2,1)} copy(bf16[192,720]{1,0:T(8,128)(2,1)} %get-tuple-element.27) | data formatting | bytes 552960
  92.1 1.5 %copy.18 = f32[7,2880]{1,0:T(8,128)} copy(f32[7,2880]{1,0:T(8,128)} %get-tuple-element.28) | data formatting | bytes 161280
Async XLA Ops:
  4.5 82.8 %copy-start = (f32[120,16]{0,1:T(8,128)S(1)}, f32[120,16]{0,1:T(8,128)}, u32[]{:S(2)}) copy-start(f32[120,16]{0,1:T(8,128)} %param.10) | copy-start | bytes 23044
